TPU v7x, 512 devices: a whole 4x4x16 slice. The times are simulated.
512 devices in a mesh: design: 16 (over y, x_lo, core), seq: 32 (over x_hi, z).
Axes of the slice: x: 4 (x_hi: 2, x_lo: 2; x = x_hi * 2 + x_lo), y: 4, z: 16, core: 2. Of those that a mesh axis runs over, the one named last changes fastest.
Arguments:
- window_x: bfloat16 [16, 512, 8192], P('design', 'seq'), may hold values from -6 to 6
- norm_gain: float32 [8192], replicated, may hold values from 0.5 to 1.5
- proj_weight: bfloat16 [8192, 3, 4096], P('design', None, 'seq'), may hold values from -0.0625 to 0.0625
- proj_tail: bfloat16 [16, 6, 3, 4096], P('design', None, None, 'seq'), may hold values from -6 to 6
- short_taps: float32 [7, 3, 4096], P(None, None, 'seq'), may hold values from -2 to 2
- decay_rates: float32 [4096, 16], replicated, may hold values from 8.680556e-06 to 0.035
- residues: float32 [4096, 16], P('seq'), may hold values from 0 to 0.03
- skip_bias: float32 [4096], P('seq'), may hold values from -6 to 6
- context_u: bfloat16 [16, 4096, 4096], P('design', 'seq'), may hold values from -6 to 6
- context_tokens: int32 [16, 4096], P('design', 'seq'), may hold values from 0 to 4, as said below
Outputs:
- mixed: bfloat16 [16, 512, 4096], P('design', None, 'seq')
Inputs may be any that keep to these rules, and one draw needn't show every extreme that they name: `context_tokens`: 0 marks padding and fills a prefix of 1 to 65 positions of each design's context; 1 to 4 are bases.
All inputs are finite; a program needn't handle non-finite values.
Results may differ from a plain program's by a relative error of at most 0.0059.
The roundings to bfloat16 on the way count: a program that leaves them out, or rounds other values in their place, can miss the bound.
Values may be sent and summed in bfloat16 or wider, within the bound.
No kernel may reach another device: no remote copies, remote signals or barrier semaphores. Data moves between devices by JAX's collectives and lax.ppermute only.
A program may use at most 128 MiB of HBM per device.

v0:
```python
import math

import jax
import jax.numpy as jnp
from jax import lax
from jax.sharding import PartitionSpec as P


def decayed_sum(values, distance, rate_table):
    columns = []
    for mode_index in range(rate_table.shape[1]):
        weights = jnp.exp(-rate_table[:, mode_index][None, :] * distance[:, None])
        columns.append(jnp.sum(values * weights, axis=0))
    return jnp.stack(columns, axis=1)


def dft_tables(length):
    indices = jnp.arange(length, dtype=jnp.int32)
    phase_int = indices[:, None] * indices[None, :] % length
    angles = phase_int.astype(jnp.float32) * (2.0 * math.pi / length)
    return (jnp.cos(angles), jnp.sin(angles))


def local(
    window_x,
    norm_gain,
    proj_weight,
    proj_tail,
    short_taps,
    decay_rates,
    residues,
    skip_bias,
    context_u,
    context_tokens,
):
    local_rows = window_x.shape[1]
    width = window_x.shape[2]
    local_chans = proj_weight.shape[2]
    seq_count = lax.axis_size("seq")
    window = local_rows * seq_count
    ctx_rows = context_u.shape[1]
    history = ctx_rows * seq_count
    seq_index = lax.axis_index("seq")
    highest = lax.Precision.HIGHEST
    rows_f = window_x[0].astype(jnp.float32)
    meansq = jnp.mean(rows_f * rows_f, axis=-1, keepdims=True)
    normed = (rows_f * lax.rsqrt(meansq + 1e-06) * norm_gain[None, :]).astype(jnp.bfloat16)
    weight_panel = lax.all_gather(proj_weight, "design", axis=0, tiled=True).reshape(
        width, 3 * local_chans
    )
    features = jnp.dot(
        lax.all_gather(normed, "seq", axis=0, tiled=True),
        weight_panel,
        preferred_element_type=jnp.float32,
    )
    features = features.astype(jnp.bfloat16).reshape(window, 3, local_chans)
    extended = jnp.concatenate([proj_tail[0], features], axis=0).astype(jnp.float32)
    filtered = jnp.zeros((window, 3, local_chans), jnp.float32)
    for tap_index in range(short_taps.shape[0]):
        begin_row = short_taps.shape[0] - 1 - tap_index
        filtered = filtered + short_taps[tap_index][None] * extended[begin_row : begin_row + window]
    queries = filtered[:, 0]
    inner_term = filtered[:, 1] * filtered[:, 2]
    rates_local = lax.dynamic_slice_in_dim(decay_rates, seq_index * local_chans, local_chans, 0)
    masked_hist = jnp.where(
        (context_tokens[0] != 0)[:, None], context_u[0], jnp.zeros((), jnp.bfloat16)
    )
    relaid = lax.all_to_all(masked_hist, "seq", split_axis=1, concat_axis=0, tiled=True)
    distance = (history - 1 - jnp.arange(history, dtype=jnp.int32)).astype(jnp.float32)
    states = decayed_sum(relaid.astype(jnp.float32), distance, rates_local)
    offsets = jnp.arange(window, dtype=jnp.int32).astype(jnp.float32)
    decay_grid = jnp.exp(-rates_local[None, :, :] * offsets[:, None, None])
    kernel = jnp.einsum("tcm,cm->tc", decay_grid, residues, precision=highest)
    carried = jnp.einsum(
        "tcm,cm->tc", decay_grid, residues * jnp.exp(-rates_local) * states, precision=highest
    )
    length = 2 * window
    cos_table, sin_table = dft_tables(length)
    zero_rows = jnp.zeros((window, local_chans), jnp.float32)

    def spectrum(values):
        padded = jnp.concatenate([values, zero_rows], axis=0)
        real_part = jnp.dot(cos_table, padded, precision=highest)
        imag_part = -jnp.dot(sin_table, padded, precision=highest)
        return (real_part, imag_part)

    inner_re, inner_im = spectrum(inner_term)
    kernel_re, kernel_im = spectrum(kernel)
    prod_re = inner_re * kernel_re - inner_im * kernel_im
    prod_im = inner_re * kernel_im + inner_im * kernel_re
    longconv = (
        jnp.dot(cos_table[:window], prod_re, precision=highest)
        - jnp.dot(sin_table[:window], prod_im, precision=highest)
    ) / length
    output_block = (queries * (longconv + carried + skip_bias[None, :] * inner_term)).astype(
        jnp.bfloat16
    )
    return output_block[None]


def solution(mesh):
    in_specs = (
        P("design", "seq", None),
        P(),
        P("design", None, "seq"),
        P("design", None, None, "seq"),
        P(None, None, "seq"),
        P(),
        P("seq", None),
        P("seq"),
        P("design", "seq", None),
        P("design", "seq"),
    )
    out_specs = P("design", None, "seq")
    return jax.shard_map(local, mesh=mesh, in_specs=in_specs, out_specs=out_specs, check_vma=False)
```

profile of v0, /device:TPU:24, one launch (start us, length us, event | category | flops | bytes accessed | tf_op | source)
XLA Modules:
  0.0 330.5 jit_solution(15777754056590807734)
XLA Ops:
  6.5 0.0 copy-start.6
  6.5 0.0 all-gather.5.cloned.1.call-start
  6.5 1.9 copy.29
  8.5 0.0 all-gather.5.cloned.1.call-update
  8.5 0.0 all-gather.3.cloned.1.call-start
  8.5 1.1 fusion.67
  9.7 1.8 fusion.69
  11.5 0.0 all-gather.3.cloned.1.call-update
  11.5 0.0 copy-start.4
  11.5 0.0 copy-start.2
  11.5 1.6 copy.31
  13.1 0.0 copy-done.6
  13.2 0.1 broadcast_select_fusion
  13.2 1.3 copy.32
  14.6 17.9 %all-to-all-start = ((bf16[128,32,128]{2,0,1:T(8,128)(2,1)}), bf16[128,32,128]{2,0,1:T(8,128)(2,1)S(1)}, u32[]{:S(2)}, u32[]{:S(2)}) async-start(bf16[128,32,128]{2,0,1:T(8,128)(2,1)} %copy.32), calls=%async_computation | async-start | bytes 2097152 | tf_op jit(solution)/shard_map/all_to_all | solution.py:68
  32.5 0.0 copy-done.4
  32.6 0.0 copy-done.2
  32.6 1.1 fusion.94
  33.8 16.2 %fusion.27 = f32[1024,1024]{1,0:T(8,128)} fusion(), kind=kLoop, calls=%fused_computation.49 | loop fusion | flops 14680064 | bytes 4194304 | tf_op jit(solution)/shard_map/cos | solution.py:21
  50.0 16.3 %fusion.26 = f32[1024,1024]{1,0:T(8,128)} fusion(), kind=kLoop, calls=%fused_computation.48 | loop fusion | flops 14680064 | bytes 4194304 | tf_op jit(solution)/shard_map/sin | solution.py:21
  66.3 18.6 %all-to-all-done = bf16[128,32,128]{2,0,1:T(8,128)(2,1)S(1)} async-done(((bf16[128,32,128]{2,0,1:T(8,128)(2,1)}), bf16[128,32,128]{2,0,1:T(8,128)(2,1)S(1)}, u32[]{:S(2)}, u32[]{:S(2)}) %all-to-all-start) | async-done | bytes 1048608 | tf_op jit(solution)/shard_map/all_to_all | solution.py:68
  85.0 0.0 copy-start.3
  85.0 5.8 %fusion.25 = (f32[128]{0:T(128)S(1)}, f32[128]{0:T(128)S(1)}, f32[128]{0:T(128)S(1)}, f32[128]{0:T(128)S(1)}, f32[128]{0:T(128)S(1)}, /*index=5*/f32[128]{0:T(12...) fusion(bf16[128,32,128]{2,0,1:T(8,128)(2,1)S(1)} %all-to-all-do, ...), kind=kLoop, calls=%fused_computation.47 | loop fusion | flops 25688064 | bytes 1081344 | tf_op jit(solution)/shard_map/reduce_sum | solution.py:13
  90.8 0.1 stack.67
  90.9 0.0 copy-done.3
  90.9 0.7 multiply_multiply_fusion
  91.6 3.1 multiply_reduce_fusion
  94.7 0.1 copy.38
  94.8 18.9 %fusion.32 = f32[1024,128]{1,0:T(8,128)S(1)} fusion(f32[512,128]{0,1:T(8,128)S(1)} %bitcast.143), kind=kOutput, calls=%fused_computation.52 | convolution fusion | flops 1625292800 | bytes 786432 | tf_op jit(solution)/shard_map/dot_general | solution.py:84
  113.7 19.2 %fusion.28 = f32[1024,128]{1,0:T(8,128)S(1)} fusion(f32[512,128]{0,1:T(8,128)S(1)} %bitcast.144), kind=kOutput, calls=%fused_computation.50 | convolution fusion | flops 1625292800 | bytes 786432 | tf_op jit(solution)/shard_map/dot_general | solution.py:83
  132.9 0.0 all-gather.5.cloned.1.call-done
  132.9 138.1 %all-gather.3.cloned.1.call-done = bf16[512,8192]{1,0:T(8,128)(2,1)} async-done(((bf16[16,8192]{1,0:T(8,128)(2,1)}), bf16[512,8192]{1,0:T(8,128)(2,1)}) %all-gather.3.cloned.1.call-update) | async-done | bytes 8388624 | tf_op jit(solution)/shard_map/all_gather | solution.py:52
  271.0 8.6 %convolution_convert_fusion = bf16[512,384]{0,1:T(8,128)(2,1)S(1)} fusion(bf16[512,8192]{1,0:T(8,128)(2,1)} %all-gather.3.cloned.1.call-done, bf16[8192,384]{0,1:T(8,128)(2,1)} %bitcast.163), kind=kOutput, calls=%fused_computation.54 | convolution fusion | flops 3221422080 | bytes 15073280 | tf_op jit(solution)/shard_map/dot_general | solution.py:51
  279.6 0.2 copy.30
  279.9 0.1 maximum_convert_fusion
  280.0 0.6 fusion.57
  280.6 19.4 %fusion.34 = f32[1024,128]{1,0:T(8,128)S(1)} fusion(f32[512,128]{1,0:T(8,128)S(1)} %fusion.78), kind=kOutput, calls=%fused_computation.53 | convolution fusion | flops 1625292800 | bytes 786432 | tf_op jit(solution)/shard_map/dot_general | solution.py:84
  300.0 0.0 copy-start.1
  300.0 18.8 %fusion.30 = f32[1024,128]{1,0:T(8,128)S(1)} fusion(f32[512,128]{1,0:T(8,128)S(1)} %fusion.78), kind=kOutput, calls=%fused_computation.51 | convolution fusion | flops 1625292800 | bytes 786432 | tf_op jit(solution)/shard_map/dot_general | solution.py:83
  318.8 0.0 copy-done.1
  318.8 0.0 copy-start
  318.8 0.0 copy-start.5
  318.8 1.8 fusion.6
  320.7 0.3 copy-done
  321.0 0.0 copy-done.5
  321.0 2.5 fusion.54
  (11 shorter events, 0.1 us)
Async XLA Ops:
  6.5 6.6 %copy-start.6 = (s32[1,128]{1,0:T(1,128)S(1)}, s32[1,128]{1,0:T(1,128)}, u32[]{:S(2)}) copy-start(s32[1,128]{1,0:T(1,128)} %param.19) | copy-start | bytes 1540
  6.5 126.4 %all-gather.5.cloned.1.call-start = ((), (), s32[]{:S(2)}) async-start(), calls=%async_computation.2 | async-start | bytes 6684672 | tf_op jit(solution)/shard_map/all_gather | solution.py:48
  8.5 262.5 %all-gather.3.cloned.1.call-start = ((), (), s32[]{:S(2)}) async-start(), calls=%async_computation.1 | async-start | bytes 8650752 | tf_op jit(solution)/shard_map/all_gather | solution.py:52
  11.5 21.1 %copy-start.4 = (bf16[1,6,3,128]{3,2,1,0:T(4,128)(2,1)S(1)}, bf16[1,6,3,128]{3,2,1,0:T(4,128)(2,1)}, u32[]{:S(2)}) copy-start(bf16[1,6,3,128]{3,2,1,0:T(4,128)(2,1)} %param.13) | copy-start | bytes 13828
  11.5 21.1 %copy-start.2 = (f32[7,3,128]{2,0,1:T(8,128)S(1)}, f32[7,3,128]{2,0,1:T(8,128)}, u32[]{:S(2)}) copy-start(f32[7,3,128]{2,0,1:T(8,128)} %param.14) | copy-start | bytes 32260
  14.6 70.4 %all-to-all-start = ((bf16[128,32,128]{2,0,1:T(8,128)(2,1)}), bf16[128,32,128]{2,0,1:T(8,128)(2,1)S(1)}, u32[]{:S(2)}, u32[]{:S(2)}) async-start(bf16[128,32,128]{2,0,1:T(8,128)(2,1)} %copy.32), calls=%async_computation | async-start | bytes 2097152 | tf_op jit(solution)/shard_map/all_to_all | solution.py:68
  85.0 5.9 %copy-start.3 = (f32[128,16]{0,1:T(8,128)S(1)}, f32[128,16]{0,1:T(8,128)}, u32[]{:S(2)}) copy-start(f32[128,16]{0,1:T(8,128)} %param.16) | copy-start | bytes 24580
  300.0 18.8 %copy-start.1 = (f32[1024,1024]{1,0:T(8,128)S(1)}, f32[1024,1024]{1,0:T(8,128)}, u32[]{:S(2)}) copy-start(f32[1024,1024]{1,0:T(8,128)} %fusion.26) | copy-start | bytes 12582916
  318.8 2.2 copy-start
  318.8 2.2 copy-start.5
Sparse Core Ops, SparseCore 0:
  9.5 62.8 all-gather.4
  75.5 195.5 all-gather.2
where the time goes:
time: 337 us; the launch traced here: 331 us
  waiting for transfers between devices  157 us (47%)
  matrix products  89.1 us (26%)
  other arithmetic  47.1 us (14%)
  starting transfers between devices  18 us (5%)
  between operations  13.9 us (4%)
  local copies, waits for them, and re-layouts  5.68 us (2%)
    all_gather x1, waiting for transfers between devices, local(): lax.all_gather(normed, 'seq', axis=0, tiled=True)  138 us
    dot_general x2, matrix products, spectrum(): imag_part = -jnp.dot(sin_table, padded, precision=highest)  38.3 us
    dot_general x2, matrix products, spectrum(): real_part = jnp.dot(cos_table, padded, precision=highest)  37.9 us
    all_to_all x1, waiting for transfers between devices, local(): lax.all_to_all(masked_hist, 'seq', split_axis=1, concat_axis=0, tiled=True)  18.6 us
    all_to_all x1, starting transfers between devices, local(): lax.all_to_all(masked_hist, 'seq', split_axis=1, concat_axis=0, tiled=True)  17.9 us
    sin x1, other arithmetic, dft_tables(): return (jnp.cos(angles), jnp.sin(angles))  16.3 us
    cos x1, other arithmetic, dft_tables(): return (jnp.cos(angles), jnp.sin(angles))  16.2 us
    dot_general x1, matrix products, local(): jnp.dot(lax.all_gather(normed, 'seq', axis=0, tiled=True), weight_panel,...  8.6 us
  transfers between devices with their start and end apart: 3, of which 2 were waited for; matrix products, arithmetic and copies ran while one was open for 26% of the time, Pallas kernels for 0%

commit v1 on v0

v1 whole, which is shorter than its diff:
```python
import functools

import jax
import jax.numpy as jnp
from jax import lax
from jax.experimental import pallas as pl
from jax.experimental.pallas import tpu as pltpu
from jax.sharding import Mesh
from jax.sharding import PartitionSpec as P

F32 = jnp.float32
BF16 = jnp.bfloat16
HALO = 8


def step(axis, size, by):
    return functools.partial(
        lax.ppermute, axis_name=axis, perm=[(i, (i + by) % size) for i in range(size)]
    )


def norm_kernel(blocks, x_ref, gain_ref, order_ref, keep_ref, give_ref):
    rows, width = x_ref.shape
    depth = width // blocks
    half = blocks // 2
    total = jnp.zeros((rows, depth), F32)
    for b in range(blocks):
        part = x_ref[:, b * depth : (b + 1) * depth].astype(F32)
        total = total + part * part
    scale = lax.rsqrt(jnp.sum(total, axis=1, keepdims=True) / width + 1e-6)
    for b in range(blocks):
        source = pl.multiple_of(order_ref[b] * depth, depth)
        part = x_ref[:, pl.ds(source, depth)].astype(F32)
        value = (part * scale * gain_ref[:, pl.ds(source, depth)]).astype(BF16)
        out_ref = keep_ref if b < half else give_ref
        place = (b % half) * depth
        out_ref[:, place : place + depth] = value


def norm(x, gain, order):
    rows, width = x.shape
    blocks = order.shape[0]
    shape = jax.ShapeDtypeStruct((rows, width // 2), BF16)
    vmem = pl.BlockSpec(memory_space=pltpu.VMEM)
    return pl.pallas_call(
        functools.partial(norm_kernel, blocks),
        out_shape=(shape, shape),
        in_specs=[vmem, vmem, pl.BlockSpec(memory_space=pltpu.SMEM)],
        out_specs=(vmem, vmem),
        compiler_params=pltpu.CompilerParams(vmem_limit_bytes=16 << 20),
        cost_estimate=pl.CostEstimate(flops=8 * rows * width, bytes_accessed=4 * rows * width, transcendentals=rows),
    )(x, gain, order)


def context_kernel(modes, u_ref, mask_ref, rates_ref, behind_ref, out_ref):
    rows, chans = u_ref.shape
    behind = behind_ref[0]
    lane = 128
    back = (7 - lax.broadcasted_iota(jnp.int32, (8, lane), 0)).astype(F32)
    back = back + behind.astype(F32)
    for at in range(0, chans, lane):
        rates = [rates_ref[m : m + 1, at : at + lane] for m in range(modes)]
        decays = [jnp.broadcast_to(jnp.exp(-8.0 * r), (8, lane)) for r in rates]
        sums = [jnp.zeros((8, lane), F32)] * modes
        for group in range(0, rows, 16):
            value = u_ref[group : group + 16, at : at + lane].astype(F32)
            value = jnp.where(mask_ref[group : group + 16, :] != 0, value, 0.0)
            for part in (value[:8], value[8:]):
                sums = [s * d + part for s, d in zip(sums, decays)]
        for m in range(modes):
            weight = jnp.exp(-rates[m] * back)
            out_ref[m : m + 1, at : at + lane] = jnp.sum(sums[m] * weight, axis=0, keepdims=True)


def context_sums(u, mask, rates, behind):
    rows, chans = u.shape
    modes = rates.shape[0]
    tile = min(chans, 512)
    return pl.pallas_call(
        functools.partial(context_kernel, modes),
        grid=(chans // tile,),
        out_shape=jax.ShapeDtypeStruct((modes, chans), F32),
        in_specs=[
            pl.BlockSpec((rows, tile), lambda i: (0, i)),
            pl.BlockSpec((rows, 128), lambda i: (0, 0)),
            pl.BlockSpec((modes, tile), lambda i: (0, i)),
            pl.BlockSpec(memory_space=pltpu.SMEM),
        ],
        out_specs=pl.BlockSpec((modes, tile), lambda i: (0, i)),
        compiler_params=pltpu.CompilerParams(vmem_limit_bytes=16 << 20),
        cost_estimate=pl.CostEstimate(flops=2 * rows * chans * modes, bytes_accessed=2 * rows * chans, transcendentals=8 * chans * modes),
    )(u, mask, rates, behind)


def finish_kernel(
    taps_count, half_ref, mine_ref, other_ref, tail_ref, taps_ref, rates_ref, res_ref, skip_ref, partial_ref,
    out_ref, ext, inner, spread,
):
    half_rows = mine_ref.shape[0]
    window = 2 * half_rows
    chans = out_ref.shape[1]
    modes = rates_ref.shape[0]
    place = pl.multiple_of(HALO + half_ref[0] * half_rows, 8)
    away = pl.multiple_of(HALO + (1 - half_ref[0]) * half_rows, 8)
    ext[0:HALO, :] = tail_ref[...]
    ext[pl.ds(place, half_rows), :] = mine_ref[...].astype(F32)
    ext[pl.ds(away, half_rows), :] = other_ref[...].astype(F32)

    rates = rates_ref[...]
    res = res_ref[...]
    decay8 = jnp.exp(-8.0 * rates)
    state = jnp.sum(partial_ref[...].astype(F32), axis=0)
    steps = [jnp.exp(-float(k) * rates) for k in range(8)]
    reads = [res * jnp.exp(-float(k + 1) * rates) for k in range(8)]
    direct = [jnp.sum(res * s, axis=0, keepdims=True) for s in steps]
    skip = skip_ref[...]

    chunk = 64
    inner[0:8, :] = jnp.zeros((8, chans), F32)
    for t in range(0, window, chunk):
        def conv(stream):
            lanes = slice(stream * chans, (stream + 1) * chans)
            total = jnp.zeros((chunk, chans), F32)
            for j in range(taps_count):
                row = HALO + t - j
                total = total + taps_ref[j : j + 1, lanes] * ext[row : row + chunk, lanes]
            return total

        inner[8 + t : 8 + t + chunk, :] = conv(1) * conv(2)
        for g in range(t, t + chunk, 8):
            fresh = state * decay8
            for k in range(8):
                folded = reads[k] * state
                spread[k, :, :] = folded[0:8] + folded[8:16]
                fresh = fresh + steps[7 - k] * inner[8 + g + k : 9 + g + k, :]
            far = jnp.sum(spread[...], axis=1)
            rows = lax.broadcasted_iota(jnp.int32, (8, chans), 0)
            near = (direct[0] + skip) * inner[8 + g : 16 + g, :]
            for k in range(1, 8):
                shifted = inner[8 + g - k : 16 + g - k, :]
                near = near + direct[k] * jnp.where(rows >= k, shifted, 0.0)
            state = fresh
            inner_out = far + near
            spread_out = inner_out
            ext[g : g + 8, 2 * chans :] = spread_out
        mixed = conv(0) * ext[t : t + chunk, 2 * chans :]
        out_ref[t : t + chunk, :] = mixed.astype(out_ref.dtype)


def finish(half, mine, other, tail, taps, rates, res, skip, partial):
    window = 2 * mine.shape[0]
    chans = mine.shape[1] // 3
    vmem = pl.BlockSpec(memory_space=pltpu.VMEM)
    return pl.pallas_call(
        functools.partial(finish_kernel, taps.shape[0]),
        out_shape=jax.ShapeDtypeStruct((window, chans), BF16),
        in_specs=[pl.BlockSpec(memory_space=pltpu.SMEM)] + [vmem] * 8,
        out_specs=vmem,
        scratch_shapes=[
            pltpu.VMEM((HALO + window, 3 * chans), F32),
            pltpu.VMEM((8 + window, chans), F32),
            pltpu.VMEM((8, 8, chans), F32),
        ],
        compiler_params=pltpu.CompilerParams(vmem_limit_bytes=24 << 20),
        cost_estimate=pl.CostEstimate(flops=60 * window * 3 * chans, bytes_accessed=8 * window * chans, transcendentals=0),
    )(half, mine, other, tail, taps, rates, res, skip, partial)


def ring_gather(block, axis, size):
    before = step(axis, size, 1)(block)
    after = step(axis, size, -1)(block)
    half = block.shape[0] // 2
    low = step(axis, size, 1)(before[:half])
    high = step(axis, size, -1)(after[half:])
    return block, before, after, low, high


def local(
    window_x, norm_gain, proj_weight, proj_tail, short_taps, decay_rates, residues, skip_bias, context_u, context_tokens
):
    y, xl, core = lax.axis_index("y"), lax.axis_index("xl"), lax.axis_index("core")
    xh, z = lax.axis_index("xh"), lax.axis_index("z")
    y_count, z_count = lax.axis_size("y"), lax.axis_size("z")
    seq_index = xh * z_count + z
    seq_count = 2 * z_count
    rows, width = window_x.shape[1:]
    depth, _, chans = proj_weight.shape
    cols = 3 * chans
    ctx_rows = context_u.shape[1]
    modes = decay_rates.shape[1]
    cross = step("core", 2, 1)

    spots = [((y + dy) % y_count) * 2 + (xl + fl) % 2 for dy in (0, y_count - 1, 1, 2) for fl in (0, 1)]
    order = jnp.stack([s * 2 + core for s in spots] + [s * 2 + 1 - core for s in spots]).astype(jnp.int32)
    keep, give = norm(window_x[0], norm_gain[None, :], order)
    took = cross(give)
    sent_rows = jnp.concatenate([keep, took], axis=0)
    all_rows = lax.all_gather(sent_rows, "z", axis=0, tiled=False)

    weight = proj_weight.reshape(depth, cols)
    near = jnp.concatenate([weight, step("xl", 2, 1)(weight)], axis=0)
    far = step("xh", 2, 1)(near)

    def panel(block):
        own, before, after, low, high = ring_gather(block, "y", y_count)
        return jnp.concatenate([own, before, after, low, high], axis=0)

    panel_near = panel(near)
    panel_far = panel(far)

    rates_t = decay_rates.T
    mask = jnp.broadcast_to(context_tokens[0][:, None], (ctx_rows, 128))
    behind = ((seq_count - 1 - seq_index) * ctx_rows)[None].astype(jnp.int32)
    sums = context_sums(context_u[0], mask, rates_t, behind)
    sums = sums.reshape(modes, seq_count, chans).transpose(1, 0, 2)
    partial = lax.all_to_all(sums, ("xh", "z"), split_axis=0, concat_axis=0, tiled=True)

    all_rows = all_rows.reshape(z_count, 2, rows, width // 2)
    theirs = all_rows[:, 1].reshape(z_count * rows, width // 2)
    ours = all_rows[:, 0].reshape(z_count * rows, width // 2)

    def dot(a, b):
        return jnp.dot(a, b, preferred_element_type=F32)

    got_far = cross(dot(theirs, panel_far))
    got_near = cross(dot(theirs, panel_near))
    features_far = (dot(ours, panel_far) + got_far).astype(BF16)
    other = step("xh", 2, 1)(features_far)
    mine = (dot(ours, panel_near) + got_near).astype(BF16)

    rates_local = lax.dynamic_slice_in_dim(rates_t, seq_index * chans, chans, 1)
    tail = proj_tail[0].reshape(-1, cols).astype(F32)
    tail = jnp.pad(tail, ((HALO - tail.shape[0], 0), (0, 0)))
    taps = short_taps.reshape(-1, cols)
    out = finish(xh[None].astype(jnp.int32), mine, other, tail, taps, rates_local, residues.T, skip_bias[None, :], partial)
    return out[None]


def solution(mesh):
    shape = mesh.devices.shape
    grid = Mesh(mesh.devices.reshape(shape[0] // 4, 2, 2, 2, shape[1] // 2), ("y", "xl", "core", "xh", "z"))
    design, seq = ("y", "xl", "core"), ("xh", "z")
    in_specs = (
        P(design, seq, None),
        P(),
        P(design, None, seq),
        P(design, None, None, seq),
        P(None, None, seq),
        P(),
        P(seq, None),
        P(seq),
        P(design, seq, None),
        P(design, seq),
    )
    return jax.shard_map(local, mesh=grid, in_specs=in_specs, out_specs=P(design, None, seq), check_vma=False)
```

time: 337 us -> 143 us (0.42); the launches traced: 331 us -> 141 us
  waiting for transfers between devices: 157 us -> 32.4 us
  matrix products: 89.1 us -> 9.02 us
  other arithmetic: 47.1 us -> 1.79 us
  starting transfers between devices: 18 us -> 60.4 us
  local copies, waits for them, and re-layouts: 5.68 us -> 16.4 us
  Pallas kernels: 0 us -> 6.99 us
    all_gather x2 -> x1, waiting for transfers between devices: 138 us -> 4.06 us  [local(): all_rows = lax.all_gather(sent_rows, 'z', axis=0, tiled=False)]
    dot_general x7 -> x4, matrix products: 89.1 us -> 9.02 us  [dot(): return jnp.dot(a, b, preferred_element_type=F32)]
    ppermute x0 -> x14, starting transfers between devices: none -> 45.5 us  [the longest x2 9.11 us: ring_gather(): low = step(axis, size, 1)(before[:half])]
    ppermute x0 -> x14, waiting for transfers between devices: none -> 28.3 us  [the longest x1 9.65 us: local(): near = jnp.concatenate([weight, step('xl', 2, 1)(weight)], axis=0)]
    all_to_all x1, waiting for transfers between devices: 18.6 us -> 0.01 us  [local(): lax.all_to_all(sums, ('xh', 'z'), split_axis=0, concat_axis=0, tiled=True)]
    sin x1 -> x0, other arithmetic: 16.3 us -> none  [dft_tables(): return (jnp.cos(angles), jnp.sin(angles))]
    cos x1 -> x0, other arithmetic: 16.2 us -> none  [dft_tables(): return (jnp.cos(angles), jnp.sin(angles))]
    pallas_call x0 -> x3, Pallas kernels: none -> 6.99 us  [the longest x1 3.67 us: context_sums(): pl.pallas_call(functools.partial(context_kernel, modes), grid=(chans // t...]
  transfers between devices with their start and end apart: 3 -> 16, of which waited for: 2 -> 7; matrix products, arithmetic and copies ran while one was open for 26% -> 17% of each run, Pallas kernels for 0% -> 3%
where the time goes in v1:
time: 143 us; the launch traced here: 141 us
  starting transfers between devices  60.4 us (42%)
  waiting for transfers between devices  32.4 us (23%)
  local copies, waits for them, and re-layouts  16.4 us (11%)
  between operations  13.8 us (10%)
  matrix products  9.02 us (6%)
  Pallas kernels  6.99 us (5%)
  other arithmetic  1.79 us (1%)
    all_to_all x1, starting transfers between devices, local(): lax.all_to_all(sums, ('xh', 'z'), split_axis=0, concat_axis=0, tiled=True)  14.9 us
    unnamed x35, local copies, waits for them, and re-layouts  10.9 us
    ppermute x1, waiting for transfers between devices, local(): near = jnp.concatenate([weight, step('xl', 2, 1)(weight)], axis=0)  9.65 us
    ppermute x2, starting transfers between devices, ring_gather(): low = step(axis, size, 1)(before[:half])  9.11 us
    dot_general x4, matrix products, dot(): return jnp.dot(a, b, preferred_element_type=F32)  9.02 us
    ppermute x2, starting transfers between devices, ring_gather(): before = step(axis, size, 1)(block)  7.83 us
    ppermute x2, waiting for transfers between devices, ring_gather(): before = step(axis, size, 1)(block)  6.86 us
    ppermute x1, starting transfers between devices, local(): other = step('xh', 2, 1)(features_far)  4.99 us
  transfers between devices with their start and end apart: 16, of which 7 were waited for; matrix products, arithmetic and copies ran while one was open for 17% of the time, Pallas kernels for 3%

profile of v1, /device:TPU:24, one launch (start us, length us, event | category | flops | bytes accessed | tf_op | source)
XLA Modules:
  0.0 140.8 jit_solution(17359799692441926682)
XLA Ops:
  6.5 0.1 stack.67.order_ref
  6.6 1.0 copy-done.2
  7.7 0.8 copy-done.3
  8.4 0.7 shard_map.100
  9.1 1.9 %collective-permute-start = (bf16[16,4096]{1,0:T(8,128)(2,1)S(1)}, bf16[16,4096]{1,0:T(8,128)(2,1)S(1)}, u32[]{:S(2)}, u32[]{:S(2)}) collective-permute-start(bf16[16,4096]{1,0:T(8,128)(2,1)S(1)} %get-tuple-element.8), channel_id=1, source_target_pairs={{0,32},{32,0},{1,33},{33,1},{2,34},{34,2},{3,35},{35,3},{4,36},{36... | collective-permute-start | bytes 393224 | tf_op jit(solution)/shard_map/ppermute | solution.py:196
  11.1 1.3 collective-permute-done
  12.4 0.7 pad_maximum_fusion.1
  13.1 0.0 all-gather.3.cloned.1.call-update
  13.1 1.2 copy.11
  14.3 3.4 %collective-permute-start.1 = (bf16[512,384]{0,1:T(8,128)(2,1)S(1)}, bf16[512,384]{0,1:T(8,128)(2,1)S(1)}, u32[]{:S(2)}, u32[]{:S(2)}) collective-permute-start(bf16[512,384]{0,1:T(8,128)(2,1)S(1)} %bitcast.61), channel_id=1, source_target_pairs={{0,64},{64,0},{1,65},{65,1},{2,66},{66,2},{3,67},{67,3},{4,68},{68... | collective-permute-start | bytes 1179656 | tf_op jit(solution)/shard_map/ppermute | solution.py:201
  17.7 9.7 %collective-permute-done.1 = bf16[512,384]{0,1:T(8,128)(2,1)S(1)} collective-permute-done((bf16[512,384]{0,1:T(8,128)(2,1)S(1)}, bf16[512,384]{0,1:T(8,128)(2,1)S(1)}, u32[]{:S(2)}, u32[]{:S(2)}) %collective-permute-start.1) | collective-permute-done | bytes 393248 | tf_op jit(solution)/shard_map/ppermute | solution.py:201
  27.4 1.1 pad_maximum_fusion
  28.4 4.9 %collective-permute-start.7 = (bf16[1024,384]{0,1:T(8,128)(2,1)}, bf16[1024,384]{0,1:T(8,128)(2,1)}, u32[]{:S(2)}, u32[]{:S(2)}) collective-permute-start(bf16[1024,384]{0,1:T(8,128)(2,1)} %pad_maximum_fusion), channel_id=1, source_target_pairs={{0,16},{16,0},{1,17},{17,1},{2,18},{18,2},{3,19},{19,3},{4,20},{20... | collective-permute-start | bytes 2359304 | tf_op jit(solution)/shard_map/ppermute | solution.py:202
  33.4 4.5 %collective-permute-start.2 = (bf16[1024,384]{0,1:T(8,128)(2,1)}, bf16[1024,384]{0,1:T(8,128)(2,1)S(1)}, u32[]{:S(2)}, u32[]{:S(2)}) collective-permute-start(bf16[1024,384]{0,1:T(8,128)(2,1)} %pad_maximum_fusion), channel_id=1, source_target_pairs={{0,128},{128,256},{256,384},{384,0},{1,129},{129,257},{257,385},{3... | collective-permute-start | bytes 2359304 | tf_op jit(solution)/shard_map/ppermute | solution.py:170
  37.9 1.9 %collective-permute-start.3 = (bf16[1024,384]{0,1:T(8,128)(2,1)}, bf16[1024,384]{0,1:T(8,128)(2,1)S(1)}, u32[]{:S(2)}, u32[]{:S(2)}) collective-permute-start(bf16[1024,384]{0,1:T(8,128)(2,1)} %pad_maximum_fusion), channel_id=1, source_target_pairs={{0,384},{128,0},{256,128},{384,256},{1,385},{129,1},{257,129},{385... | collective-permute-start | bytes 2359304 | tf_op jit(solution)/shard_map/ppermute | solution.py:171
  39.8 0.1 broadcast_in_dim.26.mask_ref
  39.9 3.7 %shard_map.101 = f32[16,4096]{1,0:T(8,128)S(1)} custom-call(bf16[128,4096]{1,0:T(8,128)(2,1)S(1)} %bitcast.53, s32[128,128]{1,0:T(8,128)S(1)} %broadcast_in_dim.26.mask_ref, f32[16,4096]{1,0:T(8,128)S(1)} %bitcast.54, s32[1]{0:T(128)} %bitcast.30.behind_ref), custom_call_target="tpu_custom_call" | custom-call | flops 16777216 | bytes 1048576 | tf_op jit(solution)/shard_map/pallas_call | solution.py:79
  43.6 0.7 bitcast_bitcast_fusion
  44.3 14.9 %all-to-all-start = ((f32[32,16,128]{2,1,0:T(8,128)}), f32[32,16,128]{2,1,0:T(8,128)S(1)}, u32[]{:S(2)}, u32[]{:S(2)}) async-start(f32[32,16,128]{2,1,0:T(8,128)} %bitcast_bitcast_fusion), calls=%async_computation | async-start | bytes 524288 | tf_op jit(solution)/shard_map/all_to_all | solution.py:216
  59.3 3.3 %collective-permute-start.8 = (bf16[1024,384]{0,1:T(8,128)(2,1)}, bf16[1024,384]{0,1:T(8,128)(2,1)}, u32[]{:S(2)}, u32[]{:S(2)}) collective-permute-start(bf16[1024,384]{0,1:T(8,128)(2,1)} %collective-permute-done.7), channel_id=1, source_target_pairs={{0,128},{128,256},{256,384},{384,0},{1,129},{129,257},{257,385},{3... | collective-permute-start | bytes 2359304 | tf_op jit(solution)/shard_map/ppermute | solution.py:170
  62.6 2.5 %collective-permute-start.9 = (bf16[1024,384]{0,1:T(8,128)(2,1)}, bf16[1024,384]{0,1:T(8,128)(2,1)S(1)}, u32[]{:S(2)}, u32[]{:S(2)}) collective-permute-start(bf16[1024,384]{0,1:T(8,128)(2,1)} %collective-permute-done.7), channel_id=1, source_target_pairs={{0,384},{128,0},{256,128},{384,256},{1,385},{129,1},{257,129},{385... | collective-permute-start | bytes 2359304 | tf_op jit(solution)/shard_map/ppermute | solution.py:171
  65.2 1.0 constant_dynamic-update-slice_fusion.4
  66.3 4.6 %collective-permute-start.4 = (bf16[512,384]{0,1:T(8,128)(2,1)S(1)}, bf16[512,384]{0,1:T(8,128)(2,1)S(1)}, u32[]{:S(2)}, u32[]{:S(2)}) collective-permute-start(bf16[512,384]{0,1:T(8,128)(2,1)S(1)} %slice.25), channel_id=1, source_target_pairs={{0,128},{128,256},{256,384},{384,0},{1,129},{129,257},{257,385},{3... | collective-permute-start | bytes 1179656 | tf_op jit(solution)/shard_map/ppermute | solution.py:173
  70.9 1.9 %collective-permute-start.5 = (bf16[512,384]{0,1:T(8,128)(2,1)S(1)}, bf16[512,384]{0,1:T(8,128)(2,1)S(1)}, u32[]{:S(2)}, u32[]{:S(2)}) collective-permute-start(bf16[512,384]{0,1:T(8,128)(2,1)S(1)} %slice.26), channel_id=1, source_target_pairs={{0,384},{128,0},{256,128},{384,256},{1,385},{129,1},{257,129},{385... | collective-permute-start | bytes 1179656 | tf_op jit(solution)/shard_map/ppermute | solution.py:174
  72.8 2.1 %constant_dynamic-update-slice_fusion.10 = bf16[4096,384]{0,1:T(8,128)(2,1)} fusion(bf16[1024,384]{0,1:T(8,128)(2,1)} %collective-permute-done.7), kind=kLoop, calls=%fused_computation.17 | loop fusion | bytes 1572864
  74.9 0.1 constant_dynamic-update-slice_fusion.3
  75.0 0.1 constant_dynamic-update-slice_fusion.2
  75.1 6.9 %collective-permute-done.8 = bf16[1024,384]{0,1:T(8,128)(2,1)} collective-permute-done((bf16[1024,384]{0,1:T(8,128)(2,1)}, bf16[1024,384]{0,1:T(8,128)(2,1)}, u32[]{:S(2)}, u32[]{:S(2)}) %collective-permute-start.8) | collective-permute-done | bytes 786464 | tf_op jit(solution)/shard_map/ppermute | solution.py:170
  81.9 1.0 slice.28
  83.0 4.6 %collective-permute-start.10 = (bf16[512,384]{0,1:T(8,128)(2,1)S(1)}, bf16[512,384]{0,1:T(8,128)(2,1)S(1)}, u32[]{:S(2)}, u32[]{:S(2)}) collective-permute-start(bf16[512,384]{0,1:T(8,128)(2,1)S(1)} %slice.28), channel_id=1, source_target_pairs={{0,128},{128,256},{256,384},{384,0},{1,129},{129,257},{257,385},{3... | collective-permute-start | bytes 1179656 | tf_op jit(solution)/shard_map/ppermute | solution.py:173
  87.5 2.7 %collective-permute-done.4 = bf16[512,384]{0,1:T(8,128)(2,1)S(1)} collective-permute-done((bf16[512,384]{0,1:T(8,128)(2,1)S(1)}, bf16[512,384]{0,1:T(8,128)(2,1)S(1)}, u32[]{:S(2)}, u32[]{:S(2)}) %collective-permute-start.4) | collective-permute-done | bytes 393248 | tf_op jit(solution)/shard_map/ppermute | solution.py:173
  90.4 2.7 %collective-permute-start.11 = (bf16[512,384]{0,1:T(8,128)(2,1)S(1)}, bf16[512,384]{0,1:T(8,128)(2,1)S(1)}, u32[]{:S(2)}, u32[]{:S(2)}) collective-permute-start(bf16[512,384]{0,1:T(8,128)(2,1)S(1)} %slice.29), channel_id=1, source_target_pairs={{0,384},{128,0},{256,128},{384,256},{1,385},{129,1},{257,129},{385... | collective-permute-start | bytes 1179656 | tf_op jit(solution)/shard_map/ppermute | solution.py:174
  93.1 2.7 %constant_dynamic-update-slice_fusion.9 = bf16[4096,384]{0,1:T(8,128)(2,1)} fusion(bf16[4096,384]{0,1:T(8,128)(2,1)} %constant_dynamic-update-slice_fusion.10, bf16[1024,384]{0,1:T(8,128)(2,1)} %collective-permute-done.8), kind=kLoop, calls=%fused_computation.16 | loop fusion | bytes 1572864
  95.8 1.0 constant_dynamic-update-slice_fusion.8
  96.8 0.8 constant_dynamic-update-slice_fusion.7
  97.6 3.7 %collective-permute-done.11 = bf16[512,384]{0,1:T(8,128)(2,1)S(1)} collective-permute-done((bf16[512,384]{0,1:T(8,128)(2,1)S(1)}, bf16[512,384]{0,1:T(8,128)(2,1)S(1)}, u32[]{:S(2)}, u32[]{:S(2)}) %collective-permute-start.11) | collective-permute-done | bytes 393248 | tf_op jit(solution)/shard_map/ppermute | solution.py:174
  101.2 0.8 constant_dynamic-update-slice_fusion.6
  102.1 4.1 %all-gather.3.cloned.1.call-done = bf16[512,4096]{1,0:T(8,128)(2,1)} async-done(((bf16[32,4096]{1,0:T(8,128)(2,1)}), bf16[512,4096]{1,0:T(8,128)(2,1)}) %all-gather.3.cloned.1.call-update) | async-done | bytes 4194320 | tf_op jit(solution)/shard_map/all_gather | solution.py:198
  106.1 2.7 %fusion.2 = (bf16[16,1,16,4096]{3,2,1,0:T(8,128)(2,1)S(1)}, bf16[16,1,16,4096]{3,2,1,0:T(8,128)(2,1)S(1)}) fusion(bf16[16,2,16,4096]{3,2,1,0:T(8,128)(2,1)} %bitcast.60), kind=kLoop, calls=%fused_computation.21 | loop fusion | bytes 8388608 | tf_op jit(solution)/shard_map/slice | solution.py:220
  108.9 3.3 %fusion.4 = f32[256,384]{1,0:T(8,128)S(1)} fusion(bf16[256,4096]{1,0:T(8,128)(2,1)S(1)} %bitcast.66, bf16[4096,384]{0,1:T(8,128)(2,1)} %constant_dynamic-update-slice_fusion.6), kind=kOutput, calls=%fused_computation.23 | convolution fusion | flops 805306368 | bytes 5636096 | tf_op jit(solution)/shard_map/dot_general | solution.py:223
  112.2 1.9 %collective-permute-start.12 = (f32[256,384]{1,0:T(8,128)S(1)}, f32[256,384]{1,0:T(8,128)S(1)}, u32[]{:S(2)}, u32[]{:S(2)}) collective-permute-start(f32[256,384]{1,0:T(8,128)S(1)} %fusion.4), channel_id=1, source_target_pairs={{0,32},{32,0},{1,33},{33,1},{2,34},{34,2},{3,35},{35,3},{4,36},{36... | collective-permute-start | bytes 1179656 | tf_op jit(solution)/shard_map/ppermute | solution.py:225
  114.1 1.3 fusion.3
  115.4 2.4 %collective-permute-start.6 = (f32[256,384]{1,0:T(8,128)S(1)}, f32[256,384]{1,0:T(8,128)S(1)}, u32[]{:S(2)}, u32[]{:S(2)}) collective-permute-start(f32[256,384]{1,0:T(8,128)S(1)} %fusion.3), channel_id=1, source_target_pairs={{0,32},{32,0},{1,33},{33,1},{2,34},{34,2},{3,35},{35,3},{4,36},{36... | collective-permute-start | bytes 1179656 | tf_op jit(solution)/shard_map/ppermute | solution.py:226
  117.8 3.2 %fusion.1 = bf16[256,384]{1,0:T(8,128)(2,1)S(1)} fusion(f32[256,384]{1,0:T(8,128)S(1)} %collective-permute-done.12, bf16[256,4096]{1,0:T(8,128)(2,1)S(1)} %bitcast.64, bf16[4096,384]{0,1:T(8,128)(2,1)} %constant_dynamic-update-slice_fusion.6), kind=kOutput, calls=%fused_computation.3 | convolution fusion | flops 805502976 | bytes 5832704 | tf_op jit(solution)/shard_map/dot_general | solution.py:223
  121.0 5.0 %collective-permute-start.13 = (bf16[256,384]{1,0:T(8,128)(2,1)S(1)}, bf16[256,384]{1,0:T(8,128)(2,1)S(1)}, u32[]{:S(2)}, u32[]{:S(2)}) collective-permute-start(bf16[256,384]{1,0:T(8,128)(2,1)S(1)} %fusion.1), channel_id=1, source_target_pairs={{0,16},{16,0},{1,17},{17,1},{2,18},{18,2},{3,19},{19,3},{4,20},{20... | collective-permute-start | bytes 589832 | tf_op jit(solution)/shard_map/ppermute | solution.py:228
  126.0 1.3 fusion.mine_ref
  127.3 4.0 %collective-permute-done.13.other_ref = bf16[256,384]{1,0:T(8,128)(2,1)S(1)} collective-permute-done((bf16[256,384]{1,0:T(8,128)(2,1)S(1)}, bf16[256,384]{1,0:T(8,128)(2,1)S(1)}, u32[]{:S(2)}, u32[]{:S(2)}) %collective-permute-start.13) | collective-permute-done | bytes 196640 | tf_op jit(solution)/shard_map/ppermute | solution.py:228
  131.4 2.6 %shard_map.102 = bf16[512,128]{1,0:T(8,128)(2,1)} custom-call(s32[1]{0:T(128)} %bitcast.half_ref, bf16[256,384]{1,0:T(8,128)(2,1)S(1)} %fusion.mine_ref, bf16[256,384]{1,0:T(8,128)(2,1)S(1)} %collective-permute-done.13.other_ref, f32[8,384]{1,0:T(8,128)S(1)} %pad_convert_fusion.tail_ref, f32[7,384]{1,0:T(8,128)S(1)} %bitcast.57, ...), custom_call_target="tpu_custom_call" | custom-call | flops 11796480 | bytes 524288 | tf_op jit(solution)/shard_map/pallas_call | solution.py:154
  (41 shorter events, 0.3 us)
Async XLA Ops:
  6.5 33.4 %copy-start = (bf16[1,128,4096]{2,1,0:T(8,128)(2,1)S(1)}, bf16[1,128,4096]{2,1,0:T(8,128)(2,1)}, u32[]{:S(2)}) copy-start(bf16[1,128,4096]{2,1,0:T(8,128)(2,1)} %param.18) | copy-start | bytes 3145732
  6.5 33.4 %copy-start.1 = (f32[4096,16]{0,1:T(8,128)S(1)}, f32[4096,16]{0,1:T(8,128)}, u32[]{:S(2)}) copy-start(f32[4096,16]{0,1:T(8,128)} %param.15) | copy-start | bytes 786436
  6.5 99.6 %all-gather.3.cloned.1.call-start = ((), (), s32[]{:S(2)}) async-start(), calls=%async_computation.1 | async-start | bytes 4456448 | tf_op jit(solution)/shard_map/all_gather | solution.py:198
  6.6 1.0 copy-start.2
  7.7 0.8 copy-start.3
  8.4 31.4 %copy-start.11 = (s32[1,128]{1,0:T(1,128)S(1)}, s32[1,128]{1,0:T(1,128)}, u32[]{:S(2)}) copy-start(s32[1,128]{1,0:T(1,128)} %param.19) | copy-start | bytes 1540
  8.4 50.8 %copy-start.10 = (bf16[1,6,3,128]{3,2,1,0:T(4,128)(2,1)S(1)}, bf16[1,6,3,128]{3,2,1,0:T(4,128)(2,1)}, u32[]{:S(2)}) copy-start(bf16[1,6,3,128]{3,2,1,0:T(4,128)(2,1)} %param.13) | copy-start | bytes 13828
  9.1 3.2 %collective-permute-start = (bf16[16,4096]{1,0:T(8,128)(2,1)S(1)}, bf16[16,4096]{1,0:T(8,128)(2,1)S(1)}, u32[]{:S(2)}, u32[]{:S(2)}) collective-permute-start(bf16[16,4096]{1,0:T(8,128)(2,1)S(1)} %get-tuple-element.8), channel_id=1, source_target_pairs={{0,32},{32,0},{1,33},{33,1},{2,34},{34,2},{3,35},{35,3},{4,36},{36... | collective-permute-start | bytes 393224 | tf_op jit(solution)/shard_map/ppermute | solution.py:196
  14.3 13.1 %collective-permute-start.1 = (bf16[512,384]{0,1:T(8,128)(2,1)S(1)}, bf16[512,384]{0,1:T(8,128)(2,1)S(1)}, u32[]{:S(2)}, u32[]{:S(2)}) collective-permute-start(bf16[512,384]{0,1:T(8,128)(2,1)S(1)} %bitcast.61), channel_id=1, source_target_pairs={{0,64},{64,0},{1,65},{65,1},{2,66},{66,2},{3,67},{67,3},{4,68},{68... | collective-permute-start | bytes 1179656 | tf_op jit(solution)/shard_map/ppermute | solution.py:201
  27.4 6.0 %copy-start.7 = (bf16[512,384]{0,1:T(8,128)(2,1)}, bf16[512,384]{0,1:T(8,128)(2,1)S(1)}, u32[]{:S(2)}) copy-start(bf16[512,384]{0,1:T(8,128)(2,1)S(1)} %collective-permute-done.1) | copy-start | bytes 1179652
  28.4 30.8 %collective-permute-start.7 = (bf16[1024,384]{0,1:T(8,128)(2,1)}, bf16[1024,384]{0,1:T(8,128)(2,1)}, u32[]{:S(2)}, u32[]{:S(2)}) collective-permute-start(bf16[1024,384]{0,1:T(8,128)(2,1)} %pad_maximum_fusion), channel_id=1, source_target_pairs={{0,16},{16,0},{1,17},{17,1},{2,18},{18,2},{3,19},{19,3},{4,20},{20... | collective-permute-start | bytes 2359304 | tf_op jit(solution)/shard_map/ppermute | solution.py:202
  33.4 32.9 %collective-permute-start.2 = (bf16[1024,384]{0,1:T(8,128)(2,1)}, bf16[1024,384]{0,1:T(8,128)(2,1)S(1)}, u32[]{:S(2)}, u32[]{:S(2)}) collective-permute-start(bf16[1024,384]{0,1:T(8,128)(2,1)} %pad_maximum_fusion), channel_id=1, source_target_pairs={{0,128},{128,256},{256,384},{384,0},{1,129},{129,257},{257,385},{3... | collective-permute-start | bytes 2359304 | tf_op jit(solution)/shard_map/ppermute | solution.py:170
  37.9 33.0 %collective-permute-start.3 = (bf16[1024,384]{0,1:T(8,128)(2,1)}, bf16[1024,384]{0,1:T(8,128)(2,1)S(1)}, u32[]{:S(2)}, u32[]{:S(2)}) collective-permute-start(bf16[1024,384]{0,1:T(8,128)(2,1)} %pad_maximum_fusion), channel_id=1, source_target_pairs={{0,384},{128,0},{256,128},{384,256},{1,385},{129,1},{257,129},{385... | collective-permute-start | bytes 2359304 | tf_op jit(solution)/shard_map/ppermute | solution.py:171
  44.3 83.0 %all-to-all-start = ((f32[32,16,128]{2,1,0:T(8,128)}), f32[32,16,128]{2,1,0:T(8,128)S(1)}, u32[]{:S(2)}, u32[]{:S(2)}) async-start(f32[32,16,128]{2,1,0:T(8,128)} %bitcast_bitcast_fusion), calls=%async_computation | async-start | bytes 524288 | tf_op jit(solution)/shard_map/all_to_all | solution.py:216
  59.3 22.7 %collective-permute-start.8 = (bf16[1024,384]{0,1:T(8,128)(2,1)}, bf16[1024,384]{0,1:T(8,128)(2,1)}, u32[]{:S(2)}, u32[]{:S(2)}) collective-permute-start(bf16[1024,384]{0,1:T(8,128)(2,1)} %collective-permute-done.7), channel_id=1, source_target_pairs={{0,128},{128,256},{256,384},{384,0},{1,129},{129,257},{257,385},{3... | collective-permute-start | bytes 2359304 | tf_op jit(solution)/shard_map/ppermute | solution.py:170
  62.6 27.7 %collective-permute-start.9 = (bf16[1024,384]{0,1:T(8,128)(2,1)}, bf16[1024,384]{0,1:T(8,128)(2,1)S(1)}, u32[]{:S(2)}, u32[]{:S(2)}) collective-permute-start(bf16[1024,384]{0,1:T(8,128)(2,1)} %collective-permute-done.7), channel_id=1, source_target_pairs={{0,384},{128,0},{256,128},{384,256},{1,385},{129,1},{257,129},{385... | collective-permute-start | bytes 2359304 | tf_op jit(solution)/shard_map/ppermute | solution.py:171
  66.3 24.0 %collective-permute-start.4 = (bf16[512,384]{0,1:T(8,128)(2,1)S(1)}, bf16[512,384]{0,1:T(8,128)(2,1)S(1)}, u32[]{:S(2)}, u32[]{:S(2)}) collective-permute-start(bf16[512,384]{0,1:T(8,128)(2,1)S(1)} %slice.25), channel_id=1, source_target_pairs={{0,128},{128,256},{256,384},{384,0},{1,129},{129,257},{257,385},{3... | collective-permute-start | bytes 1179656 | tf_op jit(solution)/shard_map/ppermute | solution.py:173
  70.9 22.1 %collective-permute-start.5 = (bf16[512,384]{0,1:T(8,128)(2,1)S(1)}, bf16[512,384]{0,1:T(8,128)(2,1)S(1)}, u32[]{:S(2)}, u32[]{:S(2)}) collective-permute-start(bf16[512,384]{0,1:T(8,128)(2,1)S(1)} %slice.26), channel_id=1, source_target_pairs={{0,384},{128,0},{256,128},{384,256},{1,385},{129,1},{257,129},{385... | collective-permute-start | bytes 1179656 | tf_op jit(solution)/shard_map/ppermute | solution.py:174
  83.0 13.8 %collective-permute-start.10 = (bf16[512,384]{0,1:T(8,128)(2,1)S(1)}, bf16[512,384]{0,1:T(8,128)(2,1)S(1)}, u32[]{:S(2)}, u32[]{:S(2)}) collective-permute-start(bf16[512,384]{0,1:T(8,128)(2,1)S(1)} %slice.28), channel_id=1, source_target_pairs={{0,128},{128,256},{256,384},{384,0},{1,129},{129,257},{257,385},{3... | collective-permute-start | bytes 1179656 | tf_op jit(solution)/shard_map/ppermute | solution.py:173
  90.4 10.9 %collective-permute-start.11 = (bf16[512,384]{0,1:T(8,128)(2,1)S(1)}, bf16[512,384]{0,1:T(8,128)(2,1)S(1)}, u32[]{:S(2)}, u32[]{:S(2)}) collective-permute-start(bf16[512,384]{0,1:T(8,128)(2,1)S(1)} %slice.29), channel_id=1, source_target_pairs={{0,384},{128,0},{256,128},{384,256},{1,385},{129,1},{257,129},{385... | collective-permute-start | bytes 1179656 | tf_op jit(solution)/shard_map/ppermute | solution.py:174
  93.1 8.2 %copy-start.8 = (bf16[4096,384]{0,1:T(8,128)(2,1)}, bf16[4096,384]{0,1:T(8,128)(2,1)S(1)}, u32[]{:S(2)}) copy-start(bf16[4096,384]{0,1:T(8,128)(2,1)S(1)} %constant_dynamic-update-slice_fusion) | copy-start | bytes 9437188
  108.8 5.2 %copy-start.9 = (bf16[4096,384]{0,1:T(8,128)(2,1)S(1)}, bf16[4096,384]{0,1:T(8,128)(2,1)}, u32[]{:S(2)}) copy-start(bf16[4096,384]{0,1:T(8,128)(2,1)} %copy-done.8) | copy-start | bytes 9437188
  112.2 5.6 %collective-permute-start.12 = (f32[256,384]{1,0:T(8,128)S(1)}, f32[256,384]{1,0:T(8,128)S(1)}, u32[]{:S(2)}, u32[]{:S(2)}) collective-permute-start(f32[256,384]{1,0:T(8,128)S(1)} %fusion.4), channel_id=1, source_target_pairs={{0,32},{32,0},{1,33},{33,1},{2,34},{34,2},{3,35},{35,3},{4,36},{36... | collective-permute-start | bytes 1179656 | tf_op jit(solution)/shard_map/ppermute | solution.py:225
  115.4 10.6 %collective-permute-start.6 = (f32[256,384]{1,0:T(8,128)S(1)}, f32[256,384]{1,0:T(8,128)S(1)}, u32[]{:S(2)}, u32[]{:S(2)}) collective-permute-start(f32[256,384]{1,0:T(8,128)S(1)} %fusion.3), channel_id=1, source_target_pairs={{0,32},{32,0},{1,33},{33,1},{2,34},{34,2},{3,35},{35,3},{4,36},{36... | collective-permute-start | bytes 1179656 | tf_op jit(solution)/shard_map/ppermute | solution.py:226
  121.0 10.4 %copy-start.4 = (f32[7,3,128]{2,0,1:T(8,128)S(1)}, f32[7,3,128]{2,0,1:T(8,128)}, u32[]{:S(2)}) copy-start(f32[7,3,128]{2,0,1:T(8,128)} %param.14) | copy-start | bytes 32260
  121.0 10.4 %copy-start.5 = (f32[128,16]{0,1:T(8,128)S(1)}, f32[128,16]{0,1:T(8,128)}, u32[]{:S(2)}) copy-start(f32[128,16]{0,1:T(8,128)} %param.16) | copy-start | bytes 24580
  121.0 10.4 %copy-start.6 = (f32[128]{0:T(128)S(1)}, f32[128]{0:T(128)}, u32[]{:S(2)}) copy-start(f32[128]{0:T(128)} %param.17) | copy-start | bytes 1540
  121.0 10.3 %collective-permute-start.13 = (bf16[256,384]{1,0:T(8,128)(2,1)S(1)}, bf16[256,384]{1,0:T(8,128)(2,1)S(1)}, u32[]{:S(2)}, u32[]{:S(2)}) collective-permute-start(bf16[256,384]{1,0:T(8,128)(2,1)S(1)} %fusion.1), channel_id=1, source_target_pairs={{0,16},{16,0},{1,17},{17,1},{2,18},{18,2},{3,19},{19,3},{4,20},{20... | collective-permute-start | bytes 589832 | tf_op jit(solution)/shard_map/ppermute | solution.py:228
Sparse Core Ops, SparseCore 0:
  13.3 92.8 all-gather.2

commit v2 on v1

--- a/solution.py
+++ b/solution.py
@@ -19,10 +19,9 @@
     )
 
 
-def norm_kernel(blocks, x_ref, gain_ref, order_ref, keep_ref, give_ref):
+def norm_kernel(blocks, x_ref, gain_ref, order_ref, out_ref):
     rows, width = x_ref.shape
     depth = width // blocks
-    half = blocks // 2
     total = jnp.zeros((rows, depth), F32)
     for b in range(blocks):
         part = x_ref[:, b * depth : (b + 1) * depth].astype(F32)
@@ -31,65 +30,68 @@
     for b in range(blocks):
         source = pl.multiple_of(order_ref[b] * depth, depth)
         part = x_ref[:, pl.ds(source, depth)].astype(F32)
-        value = (part * scale * gain_ref[:, pl.ds(source, depth)]).astype(BF16)
-        out_ref = keep_ref if b < half else give_ref
-        place = (b % half) * depth
-        out_ref[:, place : place + depth] = value
+        value = part * scale * gain_ref[:, pl.ds(source, depth)]
+        out_ref[:, b * depth : (b + 1) * depth] = value.astype(BF16)
 
 
 def norm(x, gain, order):
     rows, width = x.shape
-    blocks = order.shape[0]
-    shape = jax.ShapeDtypeStruct((rows, width // 2), BF16)
     vmem = pl.BlockSpec(memory_space=pltpu.VMEM)
     return pl.pallas_call(
-        functools.partial(norm_kernel, blocks),
-        out_shape=(shape, shape),
+        functools.partial(norm_kernel, order.shape[0]),
+        out_shape=jax.ShapeDtypeStruct((rows, width), BF16),
         in_specs=[vmem, vmem, pl.BlockSpec(memory_space=pltpu.SMEM)],
-        out_specs=(vmem, vmem),
+        out_specs=vmem,
         compiler_params=pltpu.CompilerParams(vmem_limit_bytes=16 << 20),
         cost_estimate=pl.CostEstimate(flops=8 * rows * width, bytes_accessed=4 * rows * width, transcendentals=rows),
     )(x, gain, order)
 
 
-def context_kernel(modes, u_ref, mask_ref, rates_ref, behind_ref, out_ref):
+def context_kernel(modes, where_ref, u_ref, tokens_ref, rates_ref, out_ref):
     rows, chans = u_ref.shape
-    behind = behind_ref[0]
-    lane = 128
+    lane = out_ref.shape[2]
     back = (7 - lax.broadcasted_iota(jnp.int32, (8, lane), 0)).astype(F32)
-    back = back + behind.astype(F32)
+    back = back + where_ref[1].astype(F32)
+    kept = (tokens_ref[...] != 0).astype(F32)
+    kept = jnp.broadcast_to(kept, (rows, rows)).T[:, :lane]
     for at in range(0, chans, lane):
         rates = [rates_ref[m : m + 1, at : at + lane] for m in range(modes)]
         decays = [jnp.broadcast_to(jnp.exp(-8.0 * r), (8, lane)) for r in rates]
         sums = [jnp.zeros((8, lane), F32)] * modes
         for group in range(0, rows, 16):
             value = u_ref[group : group + 16, at : at + lane].astype(F32)
-            value = jnp.where(mask_ref[group : group + 16, :] != 0, value, 0.0)
+            value = jnp.where(kept[group : group + 16, :] > 0.5, value, 0.0)
             for part in (value[:8], value[8:]):
                 sums = [s * d + part for s, d in zip(sums, decays)]
         for m in range(modes):
             weight = jnp.exp(-rates[m] * back)
-            out_ref[m : m + 1, at : at + lane] = jnp.sum(sums[m] * weight, axis=0, keepdims=True)
-
-
-def context_sums(u, mask, rates, behind):
+            out_ref[at // lane, m : m + 1, :] = jnp.sum(sums[m] * weight, axis=0, keepdims=True)
+
+
+def context_sums(u, tokens, rates, where, lane):
     rows, chans = u.shape
     modes = rates.shape[0]
-    tile = min(chans, 512)
+    blocks = chans // lane
+    each = min(4, blocks // 2)
+    tiles = blocks // each
+    tile = each * lane
+    spec = pltpu.PrefetchScalarGridSpec(
+        num_scalar_prefetch=1,
+        grid=(tiles,),
+        in_specs=[
+            pl.BlockSpec((rows, tile), lambda i, w: (0, i)),
+            pl.BlockSpec((1, rows), lambda i, w: (0, 0)),
+            pl.BlockSpec((modes, tile), lambda i, w: (0, i)),
+        ],
+        out_specs=pl.BlockSpec((each, modes, lane), lambda i, w: ((i + w[0] * (tiles // 2)) % tiles, 0, 0)),
+    )
     return pl.pallas_call(
         functools.partial(context_kernel, modes),
-        grid=(chans // tile,),
-        out_shape=jax.ShapeDtypeStruct((modes, chans), F32),
-        in_specs=[
-            pl.BlockSpec((rows, tile), lambda i: (0, i)),
-            pl.BlockSpec((rows, 128), lambda i: (0, 0)),
-            pl.BlockSpec((modes, tile), lambda i: (0, i)),
-            pl.BlockSpec(memory_space=pltpu.SMEM),
-        ],
-        out_specs=pl.BlockSpec((modes, tile), lambda i: (0, i)),
+        grid_spec=spec,
+        out_shape=jax.ShapeDtypeStruct((blocks, modes, lane), F32),
         compiler_params=pltpu.CompilerParams(vmem_limit_bytes=16 << 20),
         cost_estimate=pl.CostEstimate(flops=2 * rows * chans * modes, bytes_accessed=2 * rows * chans, transcendentals=8 * chans * modes),
-    )(u, mask, rates, behind)
+    )(where, u, tokens, rates)
 
 
 def finish_kernel(
@@ -188,51 +190,47 @@
     cols = 3 * chans
     ctx_rows = context_u.shape[1]
     modes = decay_rates.shape[1]
-    cross = step("core", 2, 1)
-
-    spots = [((y + dy) % y_count) * 2 + (xl + fl) % 2 for dy in (0, y_count - 1, 1, 2) for fl in (0, 1)]
-    order = jnp.stack([s * 2 + core for s in spots] + [s * 2 + 1 - core for s in spots]).astype(jnp.int32)
-    keep, give = norm(window_x[0], norm_gain[None, :], order)
-    took = cross(give)
-    sent_rows = jnp.concatenate([keep, took], axis=0)
-    all_rows = lax.all_gather(sent_rows, "z", axis=0, tiled=False)
+
+    order = [
+        (((y + dy) % y_count) * 2 + (xl + fl) % 2) * 2 + (xh + side) % 2
+        for fl in (0, 1) for dy in (0, y_count - 1, 1, 2) for side in (0, 1)
+    ]
+    normed = norm(window_x[0], norm_gain[None, :], jnp.stack(order).astype(jnp.int32))
+    all_rows = lax.all_gather(normed, ("z", "core"), axis=0, tiled=False)
+    all_rows = all_rows.reshape(z_count, 2, rows, width)
+
+    def swap(block, flip):
+        turned = lambda c, h: (h ^ flip[0], c ^ flip[1])
+        pairs = [(c * 2 + h, turned(c, h)[0] * 2 + turned(c, h)[1]) for c in (0, 1) for h in (0, 1)]
+        return lax.ppermute(block, ("core", "xh"), pairs)
 
     weight = proj_weight.reshape(depth, cols)
-    near = jnp.concatenate([weight, step("xl", 2, 1)(weight)], axis=0)
-    far = step("xh", 2, 1)(near)
-
-    def panel(block):
-        own, before, after, low, high = ring_gather(block, "y", y_count)
-        return jnp.concatenate([own, before, after, low, high], axis=0)
-
-    panel_near = panel(near)
-    panel_far = panel(far)
+    near = jnp.concatenate([swap(weight, (0, 0)), swap(weight, (0, 1))], axis=0)
+    far = step("xl", 2, 1)(near)
+    pieces = ring_gather(near, "y", y_count) + ring_gather(far, "y", y_count)
 
     rates_t = decay_rates.T
-    mask = jnp.broadcast_to(context_tokens[0][:, None], (ctx_rows, 128))
-    behind = ((seq_count - 1 - seq_index) * ctx_rows)[None].astype(jnp.int32)
-    sums = context_sums(context_u[0], mask, rates_t, behind)
-    sums = sums.reshape(modes, seq_count, chans).transpose(1, 0, 2)
-    partial = lax.all_to_all(sums, ("xh", "z"), split_axis=0, concat_axis=0, tiled=True)
-
-    all_rows = all_rows.reshape(z_count, 2, rows, width // 2)
-    theirs = all_rows[:, 1].reshape(z_count * rows, width // 2)
-    ours = all_rows[:, 0].reshape(z_count * rows, width // 2)
-
-    def dot(a, b):
-        return jnp.dot(a, b, preferred_element_type=F32)
-
-    got_far = cross(dot(theirs, panel_far))
-    got_near = cross(dot(theirs, panel_near))
-    features_far = (dot(ours, panel_far) + got_far).astype(BF16)
-    other = step("xh", 2, 1)(features_far)
-    mine = (dot(ours, panel_near) + got_near).astype(BF16)
+    behind = (seq_count - 1 - seq_index) * ctx_rows
+    where = jnp.stack([xh, behind]).astype(jnp.int32)
+    sums = context_sums(context_u[0], context_tokens, rates_t, where, chans)
+    sums = sums[:z_count] + step("xh", 2, 1)(sums[z_count:])
+    partial = lax.all_to_all(sums, "z", split_axis=0, concat_axis=0, tiled=True)
+
+    panel = jnp.concatenate(pieces, axis=0)
+    features = jnp.dot(all_rows.reshape(-1, width), panel, preferred_element_type=F32).astype(BF16)
+    features = features.reshape(z_count, 2, rows, cols)
+
+    def design(index):
+        return lax.dynamic_index_in_dim(features, index, 1, keepdims=False).reshape(z_count * rows, cols)
+
+    first = swap(design(xh), (0, 0))
+    second = swap(design(1 - xh), (1, 0))
 
     rates_local = lax.dynamic_slice_in_dim(rates_t, seq_index * chans, chans, 1)
     tail = proj_tail[0].reshape(-1, cols).astype(F32)
     tail = jnp.pad(tail, ((HALO - tail.shape[0], 0), (0, 0)))
     taps = short_taps.reshape(-1, cols)
-    out = finish(xh[None].astype(jnp.int32), mine, other, tail, taps, rates_local, residues.T, skip_bias[None, :], partial)
+    out = finish(core[None].astype(jnp.int32), first, second, tail, taps, rates_local, residues.T, skip_bias[None, :], partial)
     return out[None]
 
 

time: 143 us -> 132 us (0.923)
  waiting for transfers between devices: 32.4 us -> 14.5 us
  local copies, waits for them, and re-layouts: 16.4 us -> 22.8 us
  Pallas kernels: 6.99 us -> 8.46 us
    unnamed x35 -> x27, local copies, waits for them, and re-layouts: 10.9 us -> 17.9 us
    ppermute x2, waiting for transfers between devices: 6.86 us -> 0.01 us  [ring_gather(): before = step(axis, size, 1)(block)]
    ppermute x6, waiting for transfers between devices: 15 us -> 10.1 us  [the longest x4 10.1 us: swap(): return lax.ppermute(block, ('core', 'xh'), pairs)]
    all_gather x1, waiting for transfers between devices: 4.06 us -> 0.01 us  [local(): all_rows = lax.all_gather(normed, ('z', 'core'), axis=0, tiled=False)]
    ppermute x2, waiting for transfers between devices: 2.73 us -> 0.01 us  [ring_gather(): low = step(axis, size, 1)(before[:half])]
    ppermute x2, starting transfers between devices: 7.83 us -> 5.5 us  [ring_gather(): before = step(axis, size, 1)(block)]
    slice x1, local copies, waits for them, and re-layouts: 2.71 us -> 0.66 us  [local(): sums = sums[:z_count] + step('xh', 2, 1)(sums[z_count:])]
    concatenate x2 -> x0, other arithmetic: 1.78 us -> none  [the longest x1 1.05 us: local(): near = jnp.concatenate([weight, step('xl', 2, 1)(weight)], axis=0)]
  transfers between devices with their start and end apart: 16 -> 16, of which waited for: 7 -> 3; matrix products, arithmetic and copies ran while one was open for 17% -> 22% of each run, Pallas kernels for 3% -> 3%
where the time goes in v2:
time: 132 us; the launch traced here: 131 us
  starting transfers between devices  61.1 us (46%)
  local copies, waits for them, and re-layouts  22.8 us (17%)
  waiting for transfers between devices  14.5 us (11%)
  between operations  13.7 us (10%)
  matrix products  9.7 us (7%)
  Pallas kernels  8.46 us (6%)
    unnamed x27, local copies, waits for them, and re-layouts  17.9 us
    all_to_all x1, starting transfers between devices, local(): partial = lax.all_to_all(sums, 'z', split_axis=0, concat_axis=0, tiled=True)  15.2 us
    ppermute x4, starting transfers between devices, swap(): return lax.ppermute(block, ('core', 'xh'), pairs)  11.7 us
    ppermute x4, waiting for transfers between devices, swap(): return lax.ppermute(block, ('core', 'xh'), pairs)  10.1 us
    ppermute x2, starting transfers between devices, ring_gather(): low = step(axis, size, 1)(before[:half])  9.7 us
    dot_general x1, matrix products, local(): jnp.dot(all_rows.reshape(-1, width), panel, preferred_element_type=F32)  9.7 us
    ppermute x1, starting transfers between devices, local(): sums = sums[:z_count] + step('xh', 2, 1)(sums[z_count:])  6.49 us
    ppermute x2, starting transfers between devices, ring_gather(): after = step(axis, size, -1)(block)  6.19 us
  transfers between devices with their start and end apart: 16, of which 3 were waited for; matrix products, arithmetic and copies ran while one was open for 22% of the time, Pallas kernels for 3%

profile of v2, /device:TPU:24, one launch (start us, length us, event | category | flops | bytes accessed | tf_op | source)
XLA Modules:
  0.0 131.0 jit_solution(1026534377785204895)
XLA Ops:
  6.5 0.1 stack.76.order_ref
  6.6 0.9 copy-done.2
  7.6 0.8 copy-done.3
  8.3 1.4 %shard_map.100 = bf16[16,8192]{1,0:T(8,128)(2,1)} custom-call(bf16[16,8192]{1,0:T(8,128)(2,1)S(1)} %bitcast.46, f32[1,8192]{1,0:T(1,128)S(1)} %bitcast.47, s32[16]{0:T(128)S(1)} %stack.76.order_ref), custom_call_target="tpu_custom_call" | custom-call | flops 1048576 | bytes 524288 | tf_op jit(solution)/shard_map/pallas_call | solution.py:40
  9.8 1.2 copy.13
  10.9 0.7 collective-permute-start
  11.6 6.2 %collective-permute-start.1 = (bf16[512,384]{0,1:T(8,128)(2,1)S(1)}, bf16[512,384]{0,1:T(8,128)(2,1)S(1)}, u32[]{:S(2)}, u32[]{:S(2)}) collective-permute-start(bf16[512,384]{0,1:T(8,128)(2,1)S(1)} %bitcast.52), channel_id=1, source_target_pairs={{0,16},{16,48},{32,0},{48,32},{1,17},{17,49},{33,1},{49,33},{2,18}... | collective-permute-start | bytes 1179656 | tf_op jit(solution)/shard_map/ppermute | solution.py:205
  17.8 1.0 constant_dynamic-update-slice_fusion.1
  18.8 6.0 %collective-permute-done.1 = bf16[512,384]{0,1:T(8,128)(2,1)S(1)} collective-permute-done((bf16[512,384]{0,1:T(8,128)(2,1)S(1)}, bf16[512,384]{0,1:T(8,128)(2,1)S(1)}, u32[]{:S(2)}, u32[]{:S(2)}) %collective-permute-start.1) | collective-permute-done | bytes 393248 | tf_op jit(solution)/shard_map/ppermute | solution.py:205
  24.8 1.0 constant_dynamic-update-slice_fusion
  25.8 2.5 %collective-permute-start.6 = (bf16[1024,384]{0,1:T(8,128)(2,1)}, bf16[1024,384]{0,1:T(8,128)(2,1)}, u32[]{:S(2)}, u32[]{:S(2)}) collective-permute-start(bf16[1024,384]{0,1:T(8,128)(2,1)} %get-tuple-element.7), channel_id=1, source_target_pairs={{0,64},{64,0},{1,65},{65,1},{2,66},{66,2},{3,67},{67,3},{4,68},{68... | collective-permute-start | bytes 2359304 | tf_op jit(solution)/shard_map/ppermute | solution.py:209
  28.3 2.1 %collective-permute-start.2 = (bf16[1024,384]{0,1:T(8,128)(2,1)}, bf16[1024,384]{0,1:T(8,128)(2,1)S(1)}, u32[]{:S(2)}, u32[]{:S(2)}) collective-permute-start(bf16[1024,384]{0,1:T(8,128)(2,1)} %get-tuple-element.7), channel_id=1, source_target_pairs={{0,128},{128,256},{256,384},{384,0},{1,129},{129,257},{257,385},{3... | collective-permute-start | bytes 2359304 | tf_op jit(solution)/shard_map/ppermute | solution.py:172
  30.4 3.7 %collective-permute-start.3 = (bf16[1024,384]{0,1:T(8,128)(2,1)}, bf16[1024,384]{0,1:T(8,128)(2,1)S(1)}, u32[]{:S(2)}, u32[]{:S(2)}) collective-permute-start(bf16[1024,384]{0,1:T(8,128)(2,1)} %get-tuple-element.7), channel_id=1, source_target_pairs={{0,384},{128,0},{256,128},{384,256},{1,385},{129,1},{257,129},{385... | collective-permute-start | bytes 2359304 | tf_op jit(solution)/shard_map/ppermute | solution.py:173
  34.1 0.1 pad_add_fusion.where_ref
  34.2 1.2 copy-done
  35.4 0.9 copy-done.1
  36.4 0.7 copy-done.6
  37.0 4.4 %shard_map.101 = f32[32,16,128]{2,1,0:T(8,128)S(1)} custom-call(s32[2]{0:T(128)S(1)} %pad_add_fusion.where_ref, bf16[128,4096]{1,0:T(8,128)(2,1)S(1)} %bitcast.44, s32[1,128]{1,0:T(1,128)S(1)} %copy-done.6, f32[16,4096]{1,0:T(8,128)S(1)} %bitcast.45), custom_call_target="tpu_custom_call" | custom-call | flops 16777216 | bytes 1048576 | tf_op jit(solution)/shard_map/pallas_call | solution.py:88
  41.5 0.7 slice.29
  42.2 6.5 %collective-permute-start.13 = (f32[16,16,128]{2,1,0:T(8,128)}, f32[16,16,128]{2,1,0:T(8,128)S(1)}, u32[]{:S(2)}, u32[]{:S(2)}) collective-permute-start(f32[16,16,128]{2,1,0:T(8,128)} %slice.29), channel_id=1, source_target_pairs={{0,16},{16,0},{1,17},{17,1},{2,18},{18,2},{3,19},{19,3},{4,20},{20... | collective-permute-start | bytes 393224 | tf_op jit(solution)/shard_map/ppermute | solution.py:216
  48.7 3.4 %collective-permute-start.7 = (bf16[1024,384]{0,1:T(8,128)(2,1)}, bf16[1024,384]{0,1:T(8,128)(2,1)S(1)}, u32[]{:S(2)}, u32[]{:S(2)}) collective-permute-start(bf16[1024,384]{0,1:T(8,128)(2,1)} %collective-permute-done.6), channel_id=1, source_target_pairs={{0,128},{128,256},{256,384},{384,0},{1,129},{129,257},{257,385},{3... | collective-permute-start | bytes 2359304 | tf_op jit(solution)/shard_map/ppermute | solution.py:172
  52.0 2.5 %collective-permute-start.8 = (bf16[1024,384]{0,1:T(8,128)(2,1)}, bf16[1024,384]{0,1:T(8,128)(2,1)S(1)}, u32[]{:S(2)}, u32[]{:S(2)}) collective-permute-start(bf16[1024,384]{0,1:T(8,128)(2,1)} %collective-permute-done.6), channel_id=1, source_target_pairs={{0,384},{128,0},{256,128},{384,256},{1,385},{129,1},{257,129},{385... | collective-permute-start | bytes 2359304 | tf_op jit(solution)/shard_map/ppermute | solution.py:173
  54.5 0.7 copy.20
  55.2 0.8 slice.24
  56.0 4.6 %collective-permute-start.4 = (bf16[512,384]{0,1:T(8,128)(2,1)}, bf16[512,384]{0,1:T(8,128)(2,1)}, u32[]{:S(2)}, u32[]{:S(2)}) collective-permute-start(bf16[512,384]{0,1:T(8,128)(2,1)} %slice.24), channel_id=1, source_target_pairs={{0,128},{128,256},{256,384},{384,0},{1,129},{129,257},{257,385},{3... | collective-permute-start | bytes 1179656 | tf_op jit(solution)/shard_map/ppermute | solution.py:175
  60.6 0.8 slice.25
  61.4 1.9 %collective-permute-start.5 = (bf16[512,384]{0,1:T(8,128)(2,1)}, bf16[512,384]{0,1:T(8,128)(2,1)}, u32[]{:S(2)}, u32[]{:S(2)}) collective-permute-start(bf16[512,384]{0,1:T(8,128)(2,1)} %slice.25), channel_id=1, source_target_pairs={{0,384},{128,0},{256,128},{384,256},{1,385},{129,1},{257,129},{385... | collective-permute-start | bytes 1179656 | tf_op jit(solution)/shard_map/ppermute | solution.py:176
  63.3 0.7 slice_add_fusion
  64.0 15.2 %all-to-all-start = ((f32[16,16,128]{2,1,0:T(8,128)}), f32[16,16,128]{2,1,0:T(8,128)S(1)}, u32[]{:S(2)}, u32[]{:S(2)}) async-start(f32[16,16,128]{2,1,0:T(8,128)} %slice_add_fusion), calls=%async_computation | async-start | bytes 262144 | tf_op jit(solution)/shard_map/all_to_all | solution.py:217
  79.2 1.0 constant_dynamic-update-slice_fusion.10
  80.1 1.0 constant_dynamic-update-slice_fusion.9
  81.1 1.9 %constant_dynamic-update-slice_fusion.8 = bf16[8192,384]{0,1:T(8,128)(2,1)} fusion(bf16[8192,384]{0,1:T(8,128)(2,1)} %constant_dynamic-update-slice_fusion.9, bf16[512,384]{0,1:T(8,128)(2,1)} %collective-permute-done.4), kind=kLoop, calls=%fused_computation.10 | loop fusion | bytes 786432
  83.0 1.9 %constant_dynamic-update-slice_fusion.7 = bf16[8192,384]{0,1:T(8,128)(2,1)} fusion(bf16[8192,384]{0,1:T(8,128)(2,1)} %constant_dynamic-update-slice_fusion.8, bf16[512,384]{0,1:T(8,128)(2,1)} %collective-permute-done.5), kind=kLoop, calls=%fused_computation.9 | loop fusion | bytes 786432
  84.9 5.1 %collective-permute-start.9 = (bf16[512,384]{0,1:T(8,128)(2,1)S(1)}, bf16[512,384]{0,1:T(8,128)(2,1)S(1)}, u32[]{:S(2)}, u32[]{:S(2)}) collective-permute-start(bf16[512,384]{0,1:T(8,128)(2,1)S(1)} %slice.26), channel_id=1, source_target_pairs={{0,128},{128,256},{256,384},{384,0},{1,129},{129,257},{257,385},{3... | collective-permute-start | bytes 1179656 | tf_op jit(solution)/shard_map/ppermute | solution.py:175
  90.1 1.9 %collective-permute-start.10 = (bf16[512,384]{0,1:T(8,128)(2,1)S(1)}, bf16[512,384]{0,1:T(8,128)(2,1)S(1)}, u32[]{:S(2)}, u32[]{:S(2)}) collective-permute-start(bf16[512,384]{0,1:T(8,128)(2,1)S(1)} %slice.27), channel_id=1, source_target_pairs={{0,384},{128,0},{256,128},{384,256},{1,385},{129,1},{257,129},{385... | collective-permute-start | bytes 1179656 | tf_op jit(solution)/shard_map/ppermute | solution.py:176
  92.0 2.1 %constant_dynamic-update-slice_fusion.6 = bf16[8192,384]{0,1:T(8,128)(2,1)} fusion(bf16[8192,384]{0,1:T(8,128)(2,1)} %constant_dynamic-update-slice_fusion.7, bf16[1024,384]{0,1:T(8,128)(2,1)} %collective-permute-done.6), kind=kLoop, calls=%fused_computation.8 | loop fusion | bytes 1572864
  94.1 0.9 constant_dynamic-update-slice_fusion.5
  95.1 0.9 constant_dynamic-update-slice_fusion.4
  96.0 0.8 constant_dynamic-update-slice_fusion.3
  96.8 4.4 %collective-permute-done.10 = bf16[512,384]{0,1:T(8,128)(2,1)S(1)} collective-permute-done((bf16[512,384]{0,1:T(8,128)(2,1)S(1)}, bf16[512,384]{0,1:T(8,128)(2,1)S(1)}, u32[]{:S(2)}, u32[]{:S(2)}) %collective-permute-start.10) | collective-permute-done | bytes 393248 | tf_op jit(solution)/shard_map/ppermute | solution.py:176
  101.2 0.8 constant_dynamic-update-slice_fusion.2
  102.0 9.7 %convolution_convert_fusion = bf16[512,384]{1,0:T(8,128)(2,1)S(1)} fusion(bf16[512,8192]{1,0:T(8,128)(2,1)} %all-gather.3.cloned.1.call-done, bf16[8192,384]{0,1:T(8,128)(2,1)} %constant_dynamic-update-slice_fusion.2), kind=kOutput, calls=%fused_computation | convolution fusion | flops 3221422080 | bytes 15073280 | tf_op jit(solution)/shard_map/dot_general | solution.py:220
  111.7 0.1 constant_dynamic-slice_fusion
  111.8 0.7 collective-permute-start.11
  112.5 4.2 %collective-permute-start.12 = (bf16[256,384]{1,0:T(8,128)(2,1)S(1)}, bf16[256,384]{1,0:T(8,128)(2,1)S(1)}, u32[]{:S(2)}, u32[]{:S(2)}) collective-permute-start(bf16[256,384]{1,0:T(8,128)(2,1)S(1)} %bitcast.54), channel_id=1, source_target_pairs={{0,32},{16,0},{32,48},{48,16},{1,33},{17,1},{33,49},{49,17},{2,34}... | collective-permute-start | bytes 589832 | tf_op jit(solution)/shard_map/ppermute | solution.py:205
  116.7 0.7 dynamic-slice_bitcast_fusion.rates_ref
  117.4 4.1 %collective-permute-done.12.other_ref = bf16[256,384]{1,0:T(8,128)(2,1)S(1)} collective-permute-done((bf16[256,384]{1,0:T(8,128)(2,1)S(1)}, bf16[256,384]{1,0:T(8,128)(2,1)S(1)}, u32[]{:S(2)}, u32[]{:S(2)}) %collective-permute-start.12) | collective-permute-done | bytes 196640 | tf_op jit(solution)/shard_map/ppermute | solution.py:205
  121.5 2.6 %shard_map.102 = bf16[512,128]{1,0:T(8,128)(2,1)} custom-call(s32[1]{0:T(128)} %bitcast.half_ref, bf16[256,384]{1,0:T(8,128)(2,1)S(1)} %collective-permute-done.11.mine_ref, bf16[256,384]{1,0:T(8,128)(2,1)S(1)} %collective-permute-done.12.other_ref, f32[8,384]{1,0:T(8,128)S(1)} %pad_convert_fusion.tail_ref, f32[7,384]{1,0:T(8,128)S(1)} %bitcast.48, ...), custom_call_target="tpu_custom_call" | custom-call | flops 11796480 | bytes 524288 | tf_op jit(solution)/shard_map/pallas_call | solution.py:156
  (29 shorter events, 0.1 us)
Async XLA Ops:
  6.5 95.5 %all-gather.3.cloned.1.call-start = ((), (), s32[]{:S(2)}) async-start(), calls=%async_computation.1 | async-start | bytes 8650752 | tf_op jit(solution)/shard_map/all_gather | solution.py:199
  6.6 1.0 copy-start.2
  7.6 0.8 copy-start.3
  10.9 6.9 %collective-permute-start = (bf16[512,384]{0,1:T(8,128)(2,1)S(1)}, bf16[512,384]{0,1:T(8,128)(2,1)S(1)}, u32[]{:S(2)}, u32[]{:S(2)}) collective-permute-start(bf16[512,384]{0,1:T(8,128)(2,1)S(1)} %bitcast.51), channel_id=1, source_target_pairs={{0,0},{16,32},{32,16},{48,48},{1,1},{17,33},{33,17},{49,49},{2,2},... | collective-permute-start | bytes 1179656 | tf_op jit(solution)/shard_map/ppermute | solution.py:205
  11.6 13.2 %collective-permute-start.1 = (bf16[512,384]{0,1:T(8,128)(2,1)S(1)}, bf16[512,384]{0,1:T(8,128)(2,1)S(1)}, u32[]{:S(2)}, u32[]{:S(2)}) collective-permute-start(bf16[512,384]{0,1:T(8,128)(2,1)S(1)} %bitcast.52), channel_id=1, source_target_pairs={{0,16},{16,48},{32,0},{48,32},{1,17},{17,49},{33,1},{49,33},{2,18}... | collective-permute-start | bytes 1179656 | tf_op jit(solution)/shard_map/ppermute | solution.py:205
  25.8 22.9 %collective-permute-start.6 = (bf16[1024,384]{0,1:T(8,128)(2,1)}, bf16[1024,384]{0,1:T(8,128)(2,1)}, u32[]{:S(2)}, u32[]{:S(2)}) collective-permute-start(bf16[1024,384]{0,1:T(8,128)(2,1)} %get-tuple-element.7), channel_id=1, source_target_pairs={{0,64},{64,0},{1,65},{65,1},{2,66},{66,2},{3,67},{67,3},{4,68},{68... | collective-permute-start | bytes 2359304 | tf_op jit(solution)/shard_map/ppermute | solution.py:209
  28.3 27.0 %collective-permute-start.2 = (bf16[1024,384]{0,1:T(8,128)(2,1)}, bf16[1024,384]{0,1:T(8,128)(2,1)S(1)}, u32[]{:S(2)}, u32[]{:S(2)}) collective-permute-start(bf16[1024,384]{0,1:T(8,128)(2,1)} %get-tuple-element.7), channel_id=1, source_target_pairs={{0,128},{128,256},{256,384},{384,0},{1,129},{129,257},{257,385},{3... | collective-permute-start | bytes 2359304 | tf_op jit(solution)/shard_map/ppermute | solution.py:172
  30.4 30.2 %collective-permute-start.3 = (bf16[1024,384]{0,1:T(8,128)(2,1)}, bf16[1024,384]{0,1:T(8,128)(2,1)S(1)}, u32[]{:S(2)}, u32[]{:S(2)}) collective-permute-start(bf16[1024,384]{0,1:T(8,128)(2,1)} %get-tuple-element.7), channel_id=1, source_target_pairs={{0,384},{128,0},{256,128},{384,256},{1,385},{129,1},{257,129},{385... | collective-permute-start | bytes 2359304 | tf_op jit(solution)/shard_map/ppermute | solution.py:173
  34.2 1.2 copy-start
  35.4 0.9 copy-start.1
  36.4 0.7 copy-start.6
  42.2 21.1 %collective-permute-start.13 = (f32[16,16,128]{2,1,0:T(8,128)}, f32[16,16,128]{2,1,0:T(8,128)S(1)}, u32[]{:S(2)}, u32[]{:S(2)}) collective-permute-start(f32[16,16,128]{2,1,0:T(8,128)} %slice.29), channel_id=1, source_target_pairs={{0,16},{16,0},{1,17},{17,1},{2,18},{18,2},{3,19},{19,3},{4,20},{20... | collective-permute-start | bytes 393224 | tf_op jit(solution)/shard_map/ppermute | solution.py:216
  48.7 36.2 %collective-permute-start.7 = (bf16[1024,384]{0,1:T(8,128)(2,1)}, bf16[1024,384]{0,1:T(8,128)(2,1)S(1)}, u32[]{:S(2)}, u32[]{:S(2)}) collective-permute-start(bf16[1024,384]{0,1:T(8,128)(2,1)} %collective-permute-done.6), channel_id=1, source_target_pairs={{0,128},{128,256},{256,384},{384,0},{1,129},{129,257},{257,385},{3... | collective-permute-start | bytes 2359304 | tf_op jit(solution)/shard_map/ppermute | solution.py:172
  52.0 38.0 %collective-permute-start.8 = (bf16[1024,384]{0,1:T(8,128)(2,1)}, bf16[1024,384]{0,1:T(8,128)(2,1)S(1)}, u32[]{:S(2)}, u32[]{:S(2)}) collective-permute-start(bf16[1024,384]{0,1:T(8,128)(2,1)} %collective-permute-done.6), channel_id=1, source_target_pairs={{0,384},{128,0},{256,128},{384,256},{1,385},{129,1},{257,129},{385... | collective-permute-start | bytes 2359304 | tf_op jit(solution)/shard_map/ppermute | solution.py:173
  56.0 25.1 %collective-permute-start.4 = (bf16[512,384]{0,1:T(8,128)(2,1)}, bf16[512,384]{0,1:T(8,128)(2,1)}, u32[]{:S(2)}, u32[]{:S(2)}) collective-permute-start(bf16[512,384]{0,1:T(8,128)(2,1)} %slice.24), channel_id=1, source_target_pairs={{0,128},{128,256},{256,384},{384,0},{1,129},{129,257},{257,385},{3... | collective-permute-start | bytes 1179656 | tf_op jit(solution)/shard_map/ppermute | solution.py:175
  61.4 21.6 %collective-permute-start.5 = (bf16[512,384]{0,1:T(8,128)(2,1)}, bf16[512,384]{0,1:T(8,128)(2,1)}, u32[]{:S(2)}, u32[]{:S(2)}) collective-permute-start(bf16[512,384]{0,1:T(8,128)(2,1)} %slice.25), channel_id=1, source_target_pairs={{0,384},{128,0},{256,128},{384,256},{1,385},{129,1},{257,129},{385... | collective-permute-start | bytes 1179656 | tf_op jit(solution)/shard_map/ppermute | solution.py:176
  64.0 53.4 %all-to-all-start = ((f32[16,16,128]{2,1,0:T(8,128)}), f32[16,16,128]{2,1,0:T(8,128)S(1)}, u32[]{:S(2)}, u32[]{:S(2)}) async-start(f32[16,16,128]{2,1,0:T(8,128)} %slice_add_fusion), calls=%async_computation | async-start | bytes 262144 | tf_op jit(solution)/shard_map/all_to_all | solution.py:217
  84.9 11.1 %collective-permute-start.9 = (bf16[512,384]{0,1:T(8,128)(2,1)S(1)}, bf16[512,384]{0,1:T(8,128)(2,1)S(1)}, u32[]{:S(2)}, u32[]{:S(2)}) collective-permute-start(bf16[512,384]{0,1:T(8,128)(2,1)S(1)} %slice.26), channel_id=1, source_target_pairs={{0,128},{128,256},{256,384},{384,0},{1,129},{129,257},{257,385},{3... | collective-permute-start | bytes 1179656 | tf_op jit(solution)/shard_map/ppermute | solution.py:175
  90.1 11.1 %collective-permute-start.10 = (bf16[512,384]{0,1:T(8,128)(2,1)S(1)}, bf16[512,384]{0,1:T(8,128)(2,1)S(1)}, u32[]{:S(2)}, u32[]{:S(2)}) collective-permute-start(bf16[512,384]{0,1:T(8,128)(2,1)S(1)} %slice.27), channel_id=1, source_target_pairs={{0,384},{128,0},{256,128},{384,256},{1,385},{129,1},{257,129},{385... | collective-permute-start | bytes 1179656 | tf_op jit(solution)/shard_map/ppermute | solution.py:176
  102.0 19.5 %copy-start.4 = (f32[7,3,128]{2,0,1:T(8,128)S(1)}, f32[7,3,128]{2,0,1:T(8,128)}, u32[]{:S(2)}) copy-start(f32[7,3,128]{2,0,1:T(8,128)} %param.14) | copy-start | bytes 32260
  102.0 19.5 %copy-start.5 = (f32[128,16]{0,1:T(8,128)S(1)}, f32[128,16]{0,1:T(8,128)}, u32[]{:S(2)}) copy-start(f32[128,16]{0,1:T(8,128)} %param.16) | copy-start | bytes 24580
  102.0 19.5 %copy-start.7 = (f32[128]{0:T(128)S(1)}, f32[128]{0:T(128)}, u32[]{:S(2)}) copy-start(f32[128]{0:T(128)} %param.17) | copy-start | bytes 1540
  111.8 5.6 %collective-permute-start.11 = (bf16[256,384]{1,0:T(8,128)(2,1)S(1)}, bf16[256,384]{1,0:T(8,128)(2,1)S(1)}, u32[]{:S(2)}, u32[]{:S(2)}) collective-permute-start(bf16[256,384]{1,0:T(8,128)(2,1)S(1)} %bitcast.55), channel_id=1, source_target_pairs={{0,0},{16,32},{32,16},{48,48},{1,1},{17,33},{33,17},{49,49},{2,2},... | collective-permute-start | bytes 589832 | tf_op jit(solution)/shard_map/ppermute | solution.py:205
  112.5 9.1 %collective-permute-start.12 = (bf16[256,384]{1,0:T(8,128)(2,1)S(1)}, bf16[256,384]{1,0:T(8,128)(2,1)S(1)}, u32[]{:S(2)}, u32[]{:S(2)}) collective-permute-start(bf16[256,384]{1,0:T(8,128)(2,1)S(1)} %bitcast.54), channel_id=1, source_target_pairs={{0,32},{16,0},{32,48},{48,16},{1,33},{17,1},{33,49},{49,17},{2,34}... | collective-permute-start | bytes 589832 | tf_op jit(solution)/shard_map/ppermute | solution.py:205
Sparse Core Ops, SparseCore 0:
  9.9 87.8 all-gather.2

commit v3 on v2

--- a/solution.py
+++ b/solution.py
@@ -45,6 +45,71 @@
         compiler_params=pltpu.CompilerParams(vmem_limit_bytes=16 << 20),
         cost_estimate=pl.CostEstimate(flops=8 * rows * width, bytes_accessed=4 * rows * width, transcendentals=rows),
     )(x, gain, order)
+
+
+def project_kernel(first_ref, rows_ref, *refs):
+    *pieces, a_ref, b_ref, held, panel, total, row_sems, piece_sems = refs
+    chunks, depth = held.shape[0], held.shape[-1]
+    z_count, _, own_rows, cols = total.shape
+    count = z_count * 2 * own_rows
+    starts = [0]
+    for piece in pieces:
+        starts.append(starts[-1] + piece.shape[0])
+    row_copies = [
+        pltpu.make_async_copy(rows_ref.at[:, :, :, i * depth : (i + 1) * depth], held.at[i], row_sems.at[i])
+        for i in range(chunks)
+    ]
+    piece_copies = [
+        pltpu.make_async_copy(piece, panel.at[starts[p] : starts[p + 1], :], piece_sems.at[p])
+        for p, piece in enumerate(pieces)
+    ]
+    sent = 0
+    for i in range(chunks):
+        while sent < len(pieces) and starts[sent] < (i + 1) * depth:
+            piece_copies[sent].start()
+            sent += 1
+        row_copies[i].start()
+    used = 0
+    for i in range(chunks):
+        while used < len(pieces) and starts[used] < (i + 1) * depth:
+            piece_copies[used].wait()
+            used += 1
+        row_copies[i].wait()
+        rows = held[i].reshape(count, depth)
+        part = jnp.dot(rows, panel[i * depth : (i + 1) * depth, :], preferred_element_type=F32)
+        part = part.reshape(total.shape)
+        if i == 0:
+            total[...] = part
+        else:
+            total[...] += part
+    first = first_ref[0]
+    a_ref[...] = total[:, pl.ds(first, 1)].reshape(z_count * own_rows, cols).astype(a_ref.dtype)
+    b_ref[...] = total[:, pl.ds(1 - first, 1)].reshape(z_count * own_rows, cols).astype(b_ref.dtype)
+
+
+def project(first, rows, pieces):
+    z_count, designs, own_rows, width = rows.shape
+    depth, cols = pieces[0].shape
+    chunks = width // depth
+    vmem = pl.BlockSpec(memory_space=pltpu.VMEM)
+    shape = jax.ShapeDtypeStruct((z_count * own_rows, cols), BF16)
+    return pl.pallas_call(
+        project_kernel,
+        out_shape=(shape, shape),
+        in_specs=[pl.BlockSpec(memory_space=pltpu.SMEM)] + [pl.BlockSpec(memory_space=pltpu.HBM)] + [pl.BlockSpec(memory_space=pl.ANY)] * len(pieces),
+        out_specs=(vmem, vmem),
+        scratch_shapes=[
+            pltpu.VMEM((chunks, z_count, designs, own_rows, depth), BF16),
+            pltpu.VMEM((width, cols), BF16),
+            pltpu.VMEM((z_count, designs, own_rows, cols), F32),
+            pltpu.SemaphoreType.DMA((chunks,)),
+            pltpu.SemaphoreType.DMA((len(pieces),)),
+        ],
+        compiler_params=pltpu.CompilerParams(vmem_limit_bytes=56 << 20),
+        cost_estimate=pl.CostEstimate(
+            flops=4 * z_count * own_rows * width * cols, bytes_accessed=2 * width * (2 * z_count * own_rows + cols), transcendentals=0
+        ),
+    )(first, rows, *pieces)
 
 
 def context_kernel(modes, where_ref, u_ref, tokens_ref, rates_ref, out_ref):
@@ -168,13 +233,15 @@
     )(half, mine, other, tail, taps, rates, res, skip, partial)
 
 
+def ring_ends(before, after, axis, size):
+    half = before.shape[0] // 2
+    return step(axis, size, 1)(before[:half]), step(axis, size, -1)(after[half:])
+
+
 def ring_gather(block, axis, size):
     before = step(axis, size, 1)(block)
     after = step(axis, size, -1)(block)
-    half = block.shape[0] // 2
-    low = step(axis, size, 1)(before[:half])
-    high = step(axis, size, -1)(after[half:])
-    return block, before, after, low, high
+    return (block, before, after) + ring_ends(before, after, axis, size)
 
 
 def local(
@@ -207,24 +274,22 @@
     weight = proj_weight.reshape(depth, cols)
     near = jnp.concatenate([swap(weight, (0, 0)), swap(weight, (0, 1))], axis=0)
     far = step("xl", 2, 1)(near)
-    pieces = ring_gather(near, "y", y_count) + ring_gather(far, "y", y_count)
 
     rates_t = decay_rates.T
     behind = (seq_count - 1 - seq_index) * ctx_rows
     where = jnp.stack([xh, behind]).astype(jnp.int32)
     sums = context_sums(context_u[0], context_tokens, rates_t, where, chans)
+    far, sums = lax.optimization_barrier((far, sums))
+    near_pieces = ring_gather(near, "y", y_count)
     sums = sums[:z_count] + step("xh", 2, 1)(sums[z_count:])
+    before, after = (step("y", y_count, by)(far) for by in (1, -1))
+    before, after, sums = lax.optimization_barrier((before, after, sums))
+    pieces = near_pieces + (far, before, after) + ring_ends(before, after, "y", y_count)
     partial = lax.all_to_all(sums, "z", split_axis=0, concat_axis=0, tiled=True)
 
-    panel = jnp.concatenate(pieces, axis=0)
-    features = jnp.dot(all_rows.reshape(-1, width), panel, preferred_element_type=F32).astype(BF16)
-    features = features.reshape(z_count, 2, rows, cols)
-
-    def design(index):
-        return lax.dynamic_index_in_dim(features, index, 1, keepdims=False).reshape(z_count * rows, cols)
-
-    first = swap(design(xh), (0, 0))
-    second = swap(design(1 - xh), (1, 0))
+    first, second = project(xh[None].astype(jnp.int32), all_rows, pieces)
+    first = swap(first, (0, 0))
+    second = swap(second, (1, 0))
 
     rates_local = lax.dynamic_slice_in_dim(rates_t, seq_index * chans, chans, 1)
     tail = proj_tail[0].reshape(-1, cols).astype(F32)

time: 132 us -> 127 us (0.962)
  waiting for transfers between devices: 14.5 us -> 29.3 us
  local copies, waits for them, and re-layouts: 22.8 us -> 10.1 us
  matrix products: 9.7 us -> 0 us
  Pallas kernels: 8.46 us -> 16 us
  starting transfers between devices: 61.1 us -> 54.8 us
    unnamed x27 -> x29, local copies, waits for them, and re-layouts: 17.9 us -> 6.55 us
    dot_general x1 -> x0, matrix products: 9.7 us -> none  [local(): jnp.dot(all_rows.reshape(-1, width), panel, preferred_element_type=F32)]
    pallas_call x0 -> x1, Pallas kernels: none -> 7.51 us  [project(): pl.pallas_call(project_kernel, out_shape=(shape, shape), in_specs=[pl.Blo...]
    ppermute x1, waiting for transfers between devices: 0.01 us -> 6.63 us  [local(): far = step('xl', 2, 1)(near)]
    ppermute x4 -> x6, waiting for transfers between devices: 4.37 us -> 10.7 us  [the longest x2 10.7 us: local(): before, after = (step('y', y_count, by)(far) for by in (1, -1))]
    ppermute x1, starting transfers between devices: 6.49 us -> 2.25 us  [local(): sums = sums[:z_count] + step('xh', 2, 1)(sums[z_count:])]
    ppermute x4 -> x6, starting transfers between devices: 13.5 us -> 17.5 us  [the longest x2 6.05 us: ring_ends(): step(axis, size, -1)(after[half:])]
    ppermute x2 -> x1, starting transfers between devices: 5.5 us -> 2.13 us  [ring_gather(): before = step(axis, size, 1)(block)]
  transfers between devices with their start and end apart: 16 -> 16, of which waited for: 3 -> 7; matrix products, arithmetic and copies ran while one was open for 22% -> 5% of each run, Pallas kernels for 3% -> 10%
where the time goes in v3:
time: 127 us; the launch traced here: 125 us
  starting transfers between devices  54.8 us (43%)
  waiting for transfers between devices  29.3 us (23%)
  Pallas kernels  16 us (13%)
  between operations  13.7 us (11%)
  local copies, waits for them, and re-layouts  10.1 us (8%)
    all_to_all x1, starting transfers between devices, local(): partial = lax.all_to_all(sums, 'z', split_axis=0, concat_axis=0, tiled=True)  15.2 us
    ppermute x4, starting transfers between devices, swap(): return lax.ppermute(block, ('core', 'xh'), pairs)  11.5 us
    ppermute x4, waiting for transfers between devices, swap(): return lax.ppermute(block, ('core', 'xh'), pairs)  11.3 us
    ppermute x2, waiting for transfers between devices, local(): before, after = (step('y', y_count, by)(far) for by in (1, -1))  10.7 us
    pallas_call x1, Pallas kernels, project(): pl.pallas_call(project_kernel, out_shape=(shape, shape), in_specs=[pl.Blo...  7.51 us
    ppermute x1, waiting for transfers between devices, local(): far = step('xl', 2, 1)(near)  6.63 us
    unnamed x29, local copies, waits for them, and re-layouts  6.55 us
    ppermute x2, starting transfers between devices, ring_ends(): step(axis, size, -1)(after[half:])  6.05 us
  transfers between devices with their start and end apart: 16, of which 7 were waited for; matrix products, arithmetic and copies ran while one was open for 5% of the time, Pallas kernels for 10%

profile of v3, /device:TPU:24, one launch (start us, length us, event | category | flops | bytes accessed | tf_op | source)
XLA Modules:
  0.0 124.7 jit_solution(1574413526046171603)
XLA Ops:
  6.5 0.1 stack.74.order_ref
  6.6 0.0 copy-start.2
  6.6 0.9 copy-done.2
  7.6 0.8 copy-done.3
  8.3 1.4 %shard_map.100 = bf16[16,8192]{1,0:T(8,128)(2,1)} custom-call(bf16[16,8192]{1,0:T(8,128)(2,1)S(1)} %bitcast.38, f32[1,8192]{1,0:T(1,128)S(1)} %bitcast.39, s32[16]{0:T(128)S(1)} %stack.74.order_ref), custom_call_target="tpu_custom_call" | custom-call | flops 1048576 | bytes 524288 | tf_op jit(solution)/shard_map/pallas_call | solution.py:40
  9.8 0.0 all-gather.3.cloned.1.call-update
  9.8 1.2 copy.12
  11.0 0.2 copy.13
  11.2 0.7 collective-permute-start
  11.9 6.2 %collective-permute-start.1 = (bf16[512,384]{1,0:T(8,128)(2,1)S(1)}, bf16[512,384]{1,0:T(8,128)(2,1)S(1)}, u32[]{:S(2)}, u32[]{:S(2)}) collective-permute-start(bf16[512,384]{1,0:T(8,128)(2,1)S(1)} %copy.13), channel_id=1, source_target_pairs={{0,16},{16,48},{32,0},{48,32},{1,17},{17,49},{33,1},{49,33},{2,18}... | collective-permute-start | bytes 1179656 | tf_op jit(solution)/shard_map/ppermute | solution.py:272
  18.0 0.0 collective-permute-done
  18.0 0.8 constant_dynamic-update-slice_fusion.1
  18.9 6.2 %collective-permute-done.1 = bf16[512,384]{1,0:T(8,128)(2,1)S(1)} collective-permute-done((bf16[512,384]{1,0:T(8,128)(2,1)S(1)}, bf16[512,384]{1,0:T(8,128)(2,1)S(1)}, u32[]{:S(2)}, u32[]{:S(2)}) %collective-permute-start.1) | collective-permute-done | bytes 393248 | tf_op jit(solution)/shard_map/ppermute | solution.py:272
  25.0 0.8 constant_dynamic-update-slice_fusion.refs_0_
  25.8 2.5 %collective-permute-start.6 = (bf16[1024,384]{1,0:T(8,128)(2,1)}, bf16[1024,384]{1,0:T(8,128)(2,1)}, u32[]{:S(2)}, u32[]{:S(2)}) collective-permute-start(bf16[1024,384]{1,0:T(8,128)(2,1)} %constant_dynamic-update-slice_fusion.refs_0_), channel_id=1, source_target_pairs={{0,64},{64,0},{1,65},{65,1},{2,66},{66,2},{3,67},{67,3},{4,68},{68... | collective-permute-start | bytes 2359304 | tf_op jit(solution)/shard_map/ppermute | solution.py:276
  28.3 2.1 %collective-permute-start.2 = (bf16[1024,384]{1,0:T(8,128)(2,1)}, bf16[1024,384]{1,0:T(8,128)(2,1)S(1)}, u32[]{:S(2)}, u32[]{:S(2)}) collective-permute-start(bf16[1024,384]{1,0:T(8,128)(2,1)} %constant_dynamic-update-slice_fusion.refs_0_), channel_id=1, source_target_pairs={{0,128},{128,256},{256,384},{384,0},{1,129},{129,257},{257,385},{3... | collective-permute-start | bytes 2359304 | tf_op jit(solution)/shard_map/ppermute | solution.py:242
  30.5 3.7 %collective-permute-start.3 = (bf16[1024,384]{1,0:T(8,128)(2,1)}, bf16[1024,384]{1,0:T(8,128)(2,1)S(1)}, u32[]{:S(2)}, u32[]{:S(2)}) collective-permute-start(bf16[1024,384]{1,0:T(8,128)(2,1)} %constant_dynamic-update-slice_fusion.refs_0_), channel_id=1, source_target_pairs={{0,384},{128,0},{256,128},{384,256},{1,385},{129,1},{257,129},{385... | collective-permute-start | bytes 2359304 | tf_op jit(solution)/shard_map/ppermute | solution.py:243
  34.2 0.1 pad_add_fusion.where_ref
  34.3 1.2 copy-done
  35.5 0.9 copy-done.1
  36.4 0.7 copy-done.6
  37.1 4.4 %shard_map.101 = f32[32,16,128]{2,1,0:T(8,128)S(1)} custom-call(s32[2]{0:T(128)S(1)} %pad_add_fusion.where_ref, bf16[128,4096]{1,0:T(8,128)(2,1)S(1)} %bitcast.36, s32[1,128]{1,0:T(1,128)S(1)} %copy-done.6, f32[16,4096]{1,0:T(8,128)S(1)} %bitcast.37), custom_call_target="tpu_custom_call" | custom-call | flops 16777216 | bytes 1048576 | tf_op jit(solution)/shard_map/pallas_call | solution.py:153
  41.6 6.6 %collective-permute-done.6.refs_5_ = bf16[1024,384]{1,0:T(8,128)(2,1)} collective-permute-done((bf16[1024,384]{1,0:T(8,128)(2,1)}, bf16[1024,384]{1,0:T(8,128)(2,1)}, u32[]{:S(2)}, u32[]{:S(2)}) %collective-permute-start.6) | collective-permute-done | bytes 786464 | tf_op jit(solution)/shard_map/ppermute | solution.py:276
  48.2 2.1 %collective-permute-start.7 = (bf16[1024,384]{1,0:T(8,128)(2,1)}, bf16[1024,384]{1,0:T(8,128)(2,1)S(1)}, u32[]{:S(2)}, u32[]{:S(2)}) collective-permute-start(bf16[1024,384]{1,0:T(8,128)(2,1)} %collective-permute-done.6.refs_5_), channel_id=1, source_target_pairs={{0,128},{128,256},{256,384},{384,0},{1,129},{129,257},{257,385},{3... | collective-permute-start | bytes 2359304 | tf_op jit(solution)/shard_map/ppermute | solution.py:285
  50.3 3.7 %collective-permute-start.8 = (bf16[1024,384]{1,0:T(8,128)(2,1)}, bf16[1024,384]{1,0:T(8,128)(2,1)S(1)}, u32[]{:S(2)}, u32[]{:S(2)}) collective-permute-start(bf16[1024,384]{1,0:T(8,128)(2,1)} %collective-permute-done.6.refs_5_), channel_id=1, source_target_pairs={{0,384},{128,0},{256,128},{384,256},{1,385},{129,1},{257,129},{385... | collective-permute-start | bytes 2359304 | tf_op jit(solution)/shard_map/ppermute | solution.py:285
  54.1 2.3 %collective-permute-start.9 = (f32[16,16,128]{2,1,0:T(8,128)S(1)}, f32[16,16,128]{2,1,0:T(8,128)S(1)}, u32[]{:S(2)}, u32[]{:S(2)}) collective-permute-start(f32[16,16,128]{2,1,0:T(8,128)S(1)} %slice.21), channel_id=1, source_target_pairs={{0,16},{16,0},{1,17},{17,1},{2,18},{18,2},{3,19},{19,3},{4,20},{20... | collective-permute-start | bytes 393224 | tf_op jit(solution)/shard_map/ppermute | solution.py:284
  56.3 0.0 collective-permute-done.2.refs_1_
  56.4 3.3 %collective-permute-start.4 = (bf16[512,384]{1,0:T(8,128)(2,1)S(1)}, bf16[512,384]{1,0:T(8,128)(2,1)}, u32[]{:S(2)}, u32[]{:S(2)}) collective-permute-start(bf16[512,384]{1,0:T(8,128)(2,1)S(1)} %slice.24), channel_id=1, source_target_pairs={{0,128},{128,256},{256,384},{384,0},{1,129},{129,257},{257,385},{3... | collective-permute-start | bytes 1179656 | tf_op jit(solution)/shard_map/ppermute | solution.py:238
  59.7 0.0 collective-permute-done.3.refs_2_
  59.8 2.5 %collective-permute-start.5 = (bf16[512,384]{1,0:T(8,128)(2,1)S(1)}, bf16[512,384]{1,0:T(8,128)(2,1)}, u32[]{:S(2)}, u32[]{:S(2)}) collective-permute-start(bf16[512,384]{1,0:T(8,128)(2,1)S(1)} %slice.25), channel_id=1, source_target_pairs={{0,384},{128,0},{256,128},{384,256},{1,385},{129,1},{257,129},{385... | collective-permute-start | bytes 1179656 | tf_op jit(solution)/shard_map/ppermute | solution.py:238
  62.3 0.3 collective-permute-done.9
  62.7 0.7 slice_add_fusion
  63.3 7.3 %collective-permute-done.7.refs_6_ = bf16[1024,384]{1,0:T(8,128)(2,1)S(1)} collective-permute-done((bf16[1024,384]{1,0:T(8,128)(2,1)}, bf16[1024,384]{1,0:T(8,128)(2,1)S(1)}, u32[]{:S(2)}, u32[]{:S(2)}) %collective-permute-start.7) | collective-permute-done | bytes 786464 | tf_op jit(solution)/shard_map/ppermute | solution.py:285
  70.6 3.4 %collective-permute-done.8.refs_7_ = bf16[1024,384]{1,0:T(8,128)(2,1)S(1)} collective-permute-done((bf16[1024,384]{1,0:T(8,128)(2,1)}, bf16[1024,384]{1,0:T(8,128)(2,1)S(1)}, u32[]{:S(2)}, u32[]{:S(2)}) %collective-permute-start.8) | collective-permute-done | bytes 786464 | tf_op jit(solution)/shard_map/ppermute | solution.py:285
  74.0 0.9 slice.22
  74.9 2.3 %collective-permute-start.10 = (bf16[512,384]{1,0:T(8,128)(2,1)}, bf16[512,384]{1,0:T(8,128)(2,1)}, u32[]{:S(2)}, u32[]{:S(2)}) collective-permute-start(bf16[512,384]{1,0:T(8,128)(2,1)} %slice.22), channel_id=1, source_target_pairs={{0,128},{128,256},{256,384},{384,0},{1,129},{129,257},{257,385},{3... | collective-permute-start | bytes 1179656 | tf_op jit(solution)/shard_map/ppermute | solution.py:238
  77.2 0.8 slice.23
  78.0 3.6 %collective-permute-start.11 = (bf16[512,384]{1,0:T(8,128)(2,1)}, bf16[512,384]{1,0:T(8,128)(2,1)}, u32[]{:S(2)}, u32[]{:S(2)}) collective-permute-start(bf16[512,384]{1,0:T(8,128)(2,1)} %slice.23), channel_id=1, source_target_pairs={{0,384},{128,0},{256,128},{384,256},{1,385},{129,1},{257,129},{385... | collective-permute-start | bytes 1179656 | tf_op jit(solution)/shard_map/ppermute | solution.py:238
  81.6 15.2 %all-to-all-start = ((f32[16,16,128]{2,1,0:T(8,128)}), f32[16,16,128]{2,1,0:T(8,128)S(1)}, u32[]{:S(2)}, u32[]{:S(2)}) async-start(f32[16,16,128]{2,1,0:T(8,128)} %slice_add_fusion), calls=%async_computation | async-start | bytes 262144 | tf_op jit(solution)/shard_map/all_to_all | solution.py:288
  96.8 0.0 collective-permute-done.10.refs_8_
  96.8 0.0 all-gather.3.cloned.1.call-done
  96.9 7.5 %shard_map.102 = (bf16[256,384]{1,0:T(8,128)(2,1)}, bf16[256,384]{1,0:T(8,128)(2,1)}) custom-call(s32[1]{0:T(128)} %bitcast.1.first_ref, bf16[16,2,16,8192]{3,2,1,0:T(8,128)(2,1)} %bitcast.43, bf16[1024,384]{1,0:T(8,128)(2,1)} %constant_dynamic-update-slice_fusion.refs_0_, bf16[1024,384]{1,0:T(8,128)(2,1)} %copy-done.8, bf16[1024,384]{1,0:T(8,128)(2,1)} %copy-done.9, ...), custom_call_target="tpu_custom_call" | custom-call | flops 3221225472 | bytes 14680064 | tf_op jit(solution)/shard_map/pallas_call | solution.py:96
  104.4 1.6 %collective-permute-start.12 = (bf16[256,384]{1,0:T(8,128)(2,1)}, bf16[256,384]{1,0:T(8,128)(2,1)S(1)}, u32[]{:S(2)}, u32[]{:S(2)}) collective-permute-start(bf16[256,384]{1,0:T(8,128)(2,1)} %get-tuple-element.16), channel_id=1, source_target_pairs={{0,0},{16,32},{32,16},{48,48},{1,1},{17,33},{33,17},{49,49},{2,2},... | collective-permute-start | bytes 589832 | tf_op jit(solution)/shard_map/ppermute | solution.py:272
  106.0 3.1 %collective-permute-start.13 = (bf16[256,384]{1,0:T(8,128)(2,1)}, bf16[256,384]{1,0:T(8,128)(2,1)S(1)}, u32[]{:S(2)}, u32[]{:S(2)}) collective-permute-start(bf16[256,384]{1,0:T(8,128)(2,1)} %get-tuple-element.17), channel_id=1, source_target_pairs={{0,32},{16,0},{32,48},{48,16},{1,33},{17,1},{33,49},{49,17},{2,34}... | collective-permute-start | bytes 589832 | tf_op jit(solution)/shard_map/ppermute | solution.py:272
  109.1 0.7 dynamic-slice_bitcast_fusion.rates_ref
  109.8 0.4 all-to-all-done.partial_ref
  110.2 5.1 %collective-permute-done.13.other_ref = bf16[256,384]{1,0:T(8,128)(2,1)S(1)} collective-permute-done((bf16[256,384]{1,0:T(8,128)(2,1)}, bf16[256,384]{1,0:T(8,128)(2,1)S(1)}, u32[]{:S(2)}, u32[]{:S(2)}) %collective-permute-start.13) | collective-permute-done | bytes 196640 | tf_op jit(solution)/shard_map/ppermute | solution.py:272
  115.3 2.6 %shard_map.103 = bf16[512,128]{1,0:T(8,128)(2,1)} custom-call(s32[1]{0:T(128)} %bitcast.half_ref, bf16[256,384]{1,0:T(8,128)(2,1)S(1)} %collective-permute-done.12.mine_ref, bf16[256,384]{1,0:T(8,128)(2,1)S(1)} %collective-permute-done.13.other_ref, f32[8,384]{1,0:T(8,128)S(1)} %pad_convert_fusion.tail_ref, f32[7,384]{1,0:T(8,128)S(1)} %bitcast.40, ...), custom_call_target="tpu_custom_call" | custom-call | flops 11796480 | bytes 524288 | tf_op jit(solution)/shard_map/pallas_call | solution.py:221
  (30 shorter events, 0.2 us)
Async XLA Ops:
  6.5 75.0 %copy-start.12 = (bf16[1,6,3,128]{3,2,1,0:T(4,128)(2,1)S(1)}, bf16[1,6,3,128]{3,2,1,0:T(4,128)(2,1)}, u32[]{:S(2)}) copy-start(bf16[1,6,3,128]{3,2,1,0:T(4,128)(2,1)} %param.13) | copy-start | bytes 13828
  6.5 90.3 %all-gather.3.cloned.1.call-start = ((), (), s32[]{:S(2)}) async-start(), calls=%async_computation.1 | async-start | bytes 8650752 | tf_op jit(solution)/shard_map/all_gather | solution.py:266
  6.6 1.0 copy-start.2
  7.6 0.8 copy-start.3
  11.2 6.9 %collective-permute-start = (bf16[512,384]{1,0:T(8,128)(2,1)S(1)}, bf16[512,384]{1,0:T(8,128)(2,1)S(1)}, u32[]{:S(2)}, u32[]{:S(2)}) collective-permute-start(bf16[512,384]{1,0:T(8,128)(2,1)S(1)} %copy.13), channel_id=1, source_target_pairs={{0,0},{16,32},{32,16},{48,48},{1,1},{17,33},{33,17},{49,49},{2,2},... | collective-permute-start | bytes 1179656 | tf_op jit(solution)/shard_map/ppermute | solution.py:272
  11.9 13.2 %collective-permute-start.1 = (bf16[512,384]{1,0:T(8,128)(2,1)S(1)}, bf16[512,384]{1,0:T(8,128)(2,1)S(1)}, u32[]{:S(2)}, u32[]{:S(2)}) collective-permute-start(bf16[512,384]{1,0:T(8,128)(2,1)S(1)} %copy.13), channel_id=1, source_target_pairs={{0,16},{16,48},{32,0},{48,32},{1,17},{17,49},{33,1},{49,33},{2,18}... | collective-permute-start | bytes 1179656 | tf_op jit(solution)/shard_map/ppermute | solution.py:272
  25.8 22.4 %collective-permute-start.6 = (bf16[1024,384]{1,0:T(8,128)(2,1)}, bf16[1024,384]{1,0:T(8,128)(2,1)}, u32[]{:S(2)}, u32[]{:S(2)}) collective-permute-start(bf16[1024,384]{1,0:T(8,128)(2,1)} %constant_dynamic-update-slice_fusion.refs_0_), channel_id=1, source_target_pairs={{0,64},{64,0},{1,65},{65,1},{2,66},{66,2},{3,67},{67,3},{4,68},{68... | collective-permute-start | bytes 2359304 | tf_op jit(solution)/shard_map/ppermute | solution.py:276
  28.3 28.0 %collective-permute-start.2 = (bf16[1024,384]{1,0:T(8,128)(2,1)}, bf16[1024,384]{1,0:T(8,128)(2,1)S(1)}, u32[]{:S(2)}, u32[]{:S(2)}) collective-permute-start(bf16[1024,384]{1,0:T(8,128)(2,1)} %constant_dynamic-update-slice_fusion.refs_0_), channel_id=1, source_target_pairs={{0,128},{128,256},{256,384},{384,0},{1,129},{129,257},{257,385},{3... | collective-permute-start | bytes 2359304 | tf_op jit(solution)/shard_map/ppermute | solution.py:242
  30.5 29.3 %collective-permute-start.3 = (bf16[1024,384]{1,0:T(8,128)(2,1)}, bf16[1024,384]{1,0:T(8,128)(2,1)S(1)}, u32[]{:S(2)}, u32[]{:S(2)}) collective-permute-start(bf16[1024,384]{1,0:T(8,128)(2,1)} %constant_dynamic-update-slice_fusion.refs_0_), channel_id=1, source_target_pairs={{0,384},{128,0},{256,128},{384,256},{1,385},{129,1},{257,129},{385... | collective-permute-start | bytes 2359304 | tf_op jit(solution)/shard_map/ppermute | solution.py:243
  34.3 1.2 copy-start
  35.5 0.9 copy-start.1
  36.4 0.7 copy-start.6
  48.2 22.5 %collective-permute-start.7 = (bf16[1024,384]{1,0:T(8,128)(2,1)}, bf16[1024,384]{1,0:T(8,128)(2,1)S(1)}, u32[]{:S(2)}, u32[]{:S(2)}) collective-permute-start(bf16[1024,384]{1,0:T(8,128)(2,1)} %collective-permute-done.6.refs_5_), channel_id=1, source_target_pairs={{0,128},{128,256},{256,384},{384,0},{1,129},{129,257},{257,385},{3... | collective-permute-start | bytes 2359304 | tf_op jit(solution)/shard_map/ppermute | solution.py:285
  50.3 23.7 %collective-permute-start.8 = (bf16[1024,384]{1,0:T(8,128)(2,1)}, bf16[1024,384]{1,0:T(8,128)(2,1)S(1)}, u32[]{:S(2)}, u32[]{:S(2)}) collective-permute-start(bf16[1024,384]{1,0:T(8,128)(2,1)} %collective-permute-done.6.refs_5_), channel_id=1, source_target_pairs={{0,384},{128,0},{256,128},{384,256},{1,385},{129,1},{257,129},{385... | collective-permute-start | bytes 2359304 | tf_op jit(solution)/shard_map/ppermute | solution.py:285
  54.1 8.6 %collective-permute-start.9 = (f32[16,16,128]{2,1,0:T(8,128)S(1)}, f32[16,16,128]{2,1,0:T(8,128)S(1)}, u32[]{:S(2)}, u32[]{:S(2)}) collective-permute-start(f32[16,16,128]{2,1,0:T(8,128)S(1)} %slice.21), channel_id=1, source_target_pairs={{0,16},{16,0},{1,17},{17,1},{2,18},{18,2},{3,19},{19,3},{4,20},{20... | collective-permute-start | bytes 393224 | tf_op jit(solution)/shard_map/ppermute | solution.py:284
  56.3 40.5 %copy-start.8 = (bf16[1024,384]{1,0:T(8,128)(2,1)}, bf16[1024,384]{1,0:T(8,128)(2,1)S(1)}, u32[]{:S(2)}) copy-start(bf16[1024,384]{1,0:T(8,128)(2,1)S(1)} %collective-permute-done.2.refs_1_) | copy-start | bytes 2359300
  56.4 40.4 %collective-permute-start.4 = (bf16[512,384]{1,0:T(8,128)(2,1)S(1)}, bf16[512,384]{1,0:T(8,128)(2,1)}, u32[]{:S(2)}, u32[]{:S(2)}) collective-permute-start(bf16[512,384]{1,0:T(8,128)(2,1)S(1)} %slice.24), channel_id=1, source_target_pairs={{0,128},{128,256},{256,384},{384,0},{1,129},{129,257},{257,385},{3... | collective-permute-start | bytes 1179656 | tf_op jit(solution)/shard_map/ppermute | solution.py:238
  59.8 37.1 %copy-start.9 = (bf16[1024,384]{1,0:T(8,128)(2,1)}, bf16[1024,384]{1,0:T(8,128)(2,1)S(1)}, u32[]{:S(2)}) copy-start(bf16[1024,384]{1,0:T(8,128)(2,1)S(1)} %collective-permute-done.3.refs_2_) | copy-start | bytes 2359300
  59.8 37.0 %collective-permute-start.5 = (bf16[512,384]{1,0:T(8,128)(2,1)S(1)}, bf16[512,384]{1,0:T(8,128)(2,1)}, u32[]{:S(2)}, u32[]{:S(2)}) collective-permute-start(bf16[512,384]{1,0:T(8,128)(2,1)S(1)} %slice.25), channel_id=1, source_target_pairs={{0,384},{128,0},{256,128},{384,256},{1,385},{129,1},{257,129},{385... | collective-permute-start | bytes 1179656 | tf_op jit(solution)/shard_map/ppermute | solution.py:238
  63.3 51.9 %copy-start.4 = (f32[7,3,128]{2,0,1:T(8,128)S(1)}, f32[7,3,128]{2,0,1:T(8,128)}, u32[]{:S(2)}) copy-start(f32[7,3,128]{2,0,1:T(8,128)} %param.14) | copy-start | bytes 32260
  63.3 51.9 %copy-start.5 = (f32[128,16]{0,1:T(8,128)S(1)}, f32[128,16]{0,1:T(8,128)}, u32[]{:S(2)}) copy-start(f32[128,16]{0,1:T(8,128)} %param.16) | copy-start | bytes 24580
  63.3 51.9 %copy-start.7 = (f32[128]{0:T(128)S(1)}, f32[128]{0:T(128)}, u32[]{:S(2)}) copy-start(f32[128]{0:T(128)} %param.17) | copy-start | bytes 1540
  70.6 26.2 %copy-start.10 = (bf16[1024,384]{1,0:T(8,128)(2,1)}, bf16[1024,384]{1,0:T(8,128)(2,1)S(1)}, u32[]{:S(2)}) copy-start(bf16[1024,384]{1,0:T(8,128)(2,1)S(1)} %collective-permute-done.7.refs_6_) | copy-start | bytes 2359300
  74.0 3.1 %copy-start.11 = (bf16[1024,384]{1,0:T(8,128)(2,1)}, bf16[1024,384]{1,0:T(8,128)(2,1)S(1)}, u32[]{:S(2)}) copy-start(bf16[1024,384]{1,0:T(8,128)(2,1)S(1)} %collective-permute-done.8.refs_7_) | copy-start | bytes 2359300
  74.9 21.9 %collective-permute-start.10 = (bf16[512,384]{1,0:T(8,128)(2,1)}, bf16[512,384]{1,0:T(8,128)(2,1)}, u32[]{:S(2)}, u32[]{:S(2)}) collective-permute-start(bf16[512,384]{1,0:T(8,128)(2,1)} %slice.22), channel_id=1, source_target_pairs={{0,128},{128,256},{256,384},{384,0},{1,129},{129,257},{257,385},{3... | collective-permute-start | bytes 1179656 | tf_op jit(solution)/shard_map/ppermute | solution.py:238
  78.0 18.8 %collective-permute-start.11 = (bf16[512,384]{1,0:T(8,128)(2,1)}, bf16[512,384]{1,0:T(8,128)(2,1)}, u32[]{:S(2)}, u32[]{:S(2)}) collective-permute-start(bf16[512,384]{1,0:T(8,128)(2,1)} %slice.23), channel_id=1, source_target_pairs={{0,384},{128,0},{256,128},{384,256},{1,385},{129,1},{257,129},{385... | collective-permute-start | bytes 1179656 | tf_op jit(solution)/shard_map/ppermute | solution.py:238
  81.6 28.6 %all-to-all-start = ((f32[16,16,128]{2,1,0:T(8,128)}), f32[16,16,128]{2,1,0:T(8,128)S(1)}, u32[]{:S(2)}, u32[]{:S(2)}) async-start(f32[16,16,128]{2,1,0:T(8,128)} %slice_add_fusion), calls=%async_computation | async-start | bytes 262144 | tf_op jit(solution)/shard_map/all_to_all | solution.py:288
  104.4 5.7 %collective-permute-start.12 = (bf16[256,384]{1,0:T(8,128)(2,1)}, bf16[256,384]{1,0:T(8,128)(2,1)S(1)}, u32[]{:S(2)}, u32[]{:S(2)}) collective-permute-start(bf16[256,384]{1,0:T(8,128)(2,1)} %get-tuple-element.16), channel_id=1, source_target_pairs={{0,0},{16,32},{32,16},{48,48},{1,1},{17,33},{33,17},{49,49},{2,2},... | collective-permute-start | bytes 589832 | tf_op jit(solution)/shard_map/ppermute | solution.py:272
  106.0 9.3 %collective-permute-start.13 = (bf16[256,384]{1,0:T(8,128)(2,1)}, bf16[256,384]{1,0:T(8,128)(2,1)S(1)}, u32[]{:S(2)}, u32[]{:S(2)}) collective-permute-start(bf16[256,384]{1,0:T(8,128)(2,1)} %get-tuple-element.17), channel_id=1, source_target_pairs={{0,32},{16,0},{32,48},{48,16},{1,33},{17,1},{33,49},{49,17},{2,34}... | collective-permute-start | bytes 589832 | tf_op jit(solution)/shard_map/ppermute | solution.py:272
Sparse Core Ops, SparseCore 0:
  9.9 83.7 all-gather.2

commit v4 on v3

--- a/solution.py
+++ b/solution.py
@@ -283,8 +283,9 @@
     near_pieces = ring_gather(near, "y", y_count)
     sums = sums[:z_count] + step("xh", 2, 1)(sums[z_count:])
     before, after = (step("y", y_count, by)(far) for by in (1, -1))
-    before, after, sums = lax.optimization_barrier((before, after, sums))
-    pieces = near_pieces + (far, before, after) + ring_ends(before, after, "y", y_count)
+    *near_pieces, low, high, sums = lax.optimization_barrier((*near_pieces, sums))
+    far_ends = (step("xl", 2, 1)(low), step("xl", 2, 1)(high))
+    pieces = (*near_pieces, low, high, far, before, after, *far_ends)
     partial = lax.all_to_all(sums, "z", split_axis=0, concat_axis=0, tiled=True)
 
     first, second = project(xh[None].astype(jnp.int32), all_rows, pieces)

time: 127 us -> 130 us (1.024)
  the two profiles are of different devices: /device:TPU:24 before, /device:TPU:32 now
where the time goes in v4:
time: 130 us; the launch traced here: 129 us
  starting transfers between devices  58 us (45%)
  waiting for transfers between devices  32.8 us (25%)
  Pallas kernels  16 us (12%)
  between operations  13.7 us (11%)
  local copies, waits for them, and re-layouts  7.67 us (6%)
    all_to_all x1, starting transfers between devices, local(): partial = lax.all_to_all(sums, 'z', split_axis=0, concat_axis=0, tiled=True)  15.2 us
    ppermute x1, waiting for transfers between devices, ring_gather(): before = step(axis, size, 1)(block)  13.5 us
    ppermute x4, waiting for transfers between devices, swap(): return lax.ppermute(block, ('core', 'xh'), pairs)  12.7 us
    ppermute x4, starting transfers between devices, swap(): return lax.ppermute(block, ('core', 'xh'), pairs)  11.1 us
    pallas_call x1, Pallas kernels, project(): pl.pallas_call(project_kernel, out_shape=(shape, shape), in_specs=[pl.Blo...  7.51 us
    ppermute x2, starting transfers between devices, local(): before, after = (step('y', y_count, by)(far) for by in (1, -1))  7.06 us
    unnamed x29, local copies, waits for them, and re-layouts  6.51 us
    ppermute x1, waiting for transfers between devices, local(): sums = sums[:z_count] + step('xh', 2, 1)(sums[z_count:])  6.21 us
  transfers between devices with their start and end apart: 16, of which 6 were waited for; matrix products, arithmetic and copies ran while one was open for 3% of the time, Pallas kernels for 9%

profile of v4, /device:TPU:32, one launch (start us, length us, event | category | flops | bytes accessed | tf_op | source)
XLA Modules:
  0.0 128.9 jit_solution(13695978142405755286)
XLA Ops:
  6.5 0.1 stack.74.order_ref
  6.6 0.0 copy-start.2
  6.6 0.9 copy-done.2
  7.6 0.8 copy-done.3
  8.3 1.4 %shard_map.100 = bf16[16,8192]{1,0:T(8,128)(2,1)} custom-call(bf16[16,8192]{1,0:T(8,128)(2,1)S(1)} %bitcast.38, f32[1,8192]{1,0:T(1,128)S(1)} %bitcast.39, s32[16]{0:T(128)S(1)} %stack.74.order_ref), custom_call_target="tpu_custom_call" | custom-call | flops 1048576 | bytes 524288 | tf_op jit(solution)/shard_map/pallas_call | solution.py:40
  9.8 0.0 all-gather.3.cloned.1.call-update
  9.8 1.2 copy.12
  11.0 0.2 copy.13
  11.2 0.7 collective-permute-start
  11.9 6.2 %collective-permute-start.1 = (bf16[512,384]{1,0:T(8,128)(2,1)S(1)}, bf16[512,384]{1,0:T(8,128)(2,1)S(1)}, u32[]{:S(2)}, u32[]{:S(2)}) collective-permute-start(bf16[512,384]{1,0:T(8,128)(2,1)S(1)} %copy.13), channel_id=1, source_target_pairs={{0,16},{16,48},{32,0},{48,32},{1,17},{17,49},{33,1},{49,33},{2,18}... | collective-permute-start | bytes 1179656 | tf_op jit(solution)/shard_map/ppermute | solution.py:272
  18.1 6.9 %collective-permute-done.1 = bf16[512,384]{1,0:T(8,128)(2,1)S(1)} collective-permute-done((bf16[512,384]{1,0:T(8,128)(2,1)S(1)}, bf16[512,384]{1,0:T(8,128)(2,1)S(1)}, u32[]{:S(2)}, u32[]{:S(2)}) %collective-permute-start.1) | collective-permute-done | bytes 393248 | tf_op jit(solution)/shard_map/ppermute | solution.py:272
  25.0 0.1 constant_dynamic-update-slice_fusion.refs_0_
  25.1 3.5 %collective-permute-start.2 = (bf16[1024,384]{1,0:T(8,128)(2,1)S(1)}, bf16[1024,384]{1,0:T(8,128)(2,1)S(1)}, u32[]{:S(2)}, u32[]{:S(2)}) collective-permute-start(bf16[1024,384]{1,0:T(8,128)(2,1)S(1)} %constant_dynamic-update-slice_fusion.refs_0_), channel_id=1, source_target_pairs={{0,128},{128,256},{256,384},{384,0},{1,129},{129,257},{257,385},{3... | collective-permute-start | bytes 2359304 | tf_op jit(solution)/shard_map/ppermute | solution.py:242
  28.6 3.6 %collective-permute-start.3 = (bf16[1024,384]{1,0:T(8,128)(2,1)S(1)}, bf16[1024,384]{1,0:T(8,128)(2,1)S(1)}, u32[]{:S(2)}, u32[]{:S(2)}) collective-permute-start(bf16[1024,384]{1,0:T(8,128)(2,1)S(1)} %constant_dynamic-update-slice_fusion.refs_0_), channel_id=1, source_target_pairs={{0,384},{128,0},{256,128},{384,256},{1,385},{129,1},{257,129},{385... | collective-permute-start | bytes 2359304 | tf_op jit(solution)/shard_map/ppermute | solution.py:243
  32.2 2.5 %collective-permute-start.6 = (bf16[1024,384]{1,0:T(8,128)(2,1)S(1)}, bf16[1024,384]{1,0:T(8,128)(2,1)}, u32[]{:S(2)}, u32[]{:S(2)}) collective-permute-start(bf16[1024,384]{1,0:T(8,128)(2,1)S(1)} %constant_dynamic-update-slice_fusion.refs_0_), channel_id=1, source_target_pairs={{0,64},{64,0},{1,65},{65,1},{2,66},{66,2},{3,67},{67,3},{4,68},{68... | collective-permute-start | bytes 2359304 | tf_op jit(solution)/shard_map/ppermute | solution.py:276
  34.7 0.1 pad_add_fusion.where_ref
  34.8 13.5 %collective-permute-done.2.refs_1_ = bf16[1024,384]{1,0:T(8,128)(2,1)S(1)} collective-permute-done((bf16[1024,384]{1,0:T(8,128)(2,1)S(1)}, bf16[1024,384]{1,0:T(8,128)(2,1)S(1)}, u32[]{:S(2)}, u32[]{:S(2)}) %collective-permute-start.2) | collective-permute-done | bytes 786464 | tf_op jit(solution)/shard_map/ppermute | solution.py:242
  48.3 2.3 %collective-permute-start.4 = (bf16[512,384]{1,0:T(8,128)(2,1)S(1)}, bf16[512,384]{1,0:T(8,128)(2,1)S(1)}, u32[]{:S(2)}, u32[]{:S(2)}) collective-permute-start(bf16[512,384]{1,0:T(8,128)(2,1)S(1)} %slice.16), channel_id=1, source_target_pairs={{0,128},{128,256},{256,384},{384,0},{1,129},{129,257},{257,385},{3... | collective-permute-start | bytes 1179656 | tf_op jit(solution)/shard_map/ppermute | solution.py:238
  50.7 0.2 collective-permute-done.3.refs_2_
  50.9 4.8 %collective-permute-start.5 = (bf16[512,384]{1,0:T(8,128)(2,1)S(1)}, bf16[512,384]{1,0:T(8,128)(2,1)S(1)}, u32[]{:S(2)}, u32[]{:S(2)}) collective-permute-start(bf16[512,384]{1,0:T(8,128)(2,1)S(1)} %slice.17), channel_id=1, source_target_pairs={{0,384},{128,0},{256,128},{384,256},{1,385},{129,1},{257,129},{385... | collective-permute-start | bytes 1179656 | tf_op jit(solution)/shard_map/ppermute | solution.py:238
  55.7 0.0 copy-start
  55.7 1.3 copy-done
  57.0 1.0 copy-done.1
  57.9 0.7 copy-done.6
  58.6 4.4 %shard_map.101 = f32[32,16,128]{2,1,0:T(8,128)S(1)} custom-call(s32[2]{0:T(128)S(1)} %pad_add_fusion.where_ref, bf16[128,4096]{1,0:T(8,128)(2,1)S(1)} %bitcast.36, s32[1,128]{1,0:T(1,128)S(1)} %copy-done.6, f32[16,4096]{1,0:T(8,128)S(1)} %bitcast.37), custom_call_target="tpu_custom_call" | custom-call | flops 16777216 | bytes 1048576 | tf_op jit(solution)/shard_map/pallas_call | solution.py:153
  63.0 0.0 collective-permute-done.6.refs_5_
  63.0 1.9 %collective-permute-start.8 = (bf16[1024,384]{1,0:T(8,128)(2,1)}, bf16[1024,384]{1,0:T(8,128)(2,1)}, u32[]{:S(2)}, u32[]{:S(2)}) collective-permute-start(bf16[1024,384]{1,0:T(8,128)(2,1)} %collective-permute-done.6.refs_5_), channel_id=1, source_target_pairs={{0,128},{128,256},{256,384},{384,0},{1,129},{129,257},{257,385},{3... | collective-permute-start | bytes 2359304 | tf_op jit(solution)/shard_map/ppermute | solution.py:285
  65.0 5.1 %collective-permute-start.9 = (bf16[1024,384]{1,0:T(8,128)(2,1)}, bf16[1024,384]{1,0:T(8,128)(2,1)}, u32[]{:S(2)}, u32[]{:S(2)}) collective-permute-start(bf16[1024,384]{1,0:T(8,128)(2,1)} %collective-permute-done.6.refs_5_), channel_id=1, source_target_pairs={{0,384},{128,0},{256,128},{384,256},{1,385},{129,1},{257,129},{385... | collective-permute-start | bytes 2359304 | tf_op jit(solution)/shard_map/ppermute | solution.py:285
  70.1 2.2 %collective-permute-start.7 = (f32[16,16,128]{2,1,0:T(8,128)S(1)}, f32[16,16,128]{2,1,0:T(8,128)S(1)}, u32[]{:S(2)}, u32[]{:S(2)}) collective-permute-start(f32[16,16,128]{2,1,0:T(8,128)S(1)} %slice.15), channel_id=1, source_target_pairs={{0,16},{16,0},{1,17},{17,1},{2,18},{18,2},{3,19},{19,3},{4,20},{20... | collective-permute-start | bytes 393224 | tf_op jit(solution)/shard_map/ppermute | solution.py:284
  72.3 6.2 %collective-permute-done.7 = f32[16,16,128]{2,1,0:T(8,128)S(1)} collective-permute-done((f32[16,16,128]{2,1,0:T(8,128)S(1)}, f32[16,16,128]{2,1,0:T(8,128)S(1)}, u32[]{:S(2)}, u32[]{:S(2)}) %collective-permute-start.7) | collective-permute-done | bytes 131104 | tf_op jit(solution)/shard_map/ppermute | solution.py:284
  78.5 0.7 slice_add_fusion
  79.2 0.0 collective-permute-done.4.refs_3_
  79.2 0.0 collective-permute-done.5.refs_4_
  79.2 2.1 %collective-permute-start.10 = (bf16[512,384]{1,0:T(8,128)(2,1)S(1)}, bf16[512,384]{1,0:T(8,128)(2,1)}, u32[]{:S(2)}, u32[]{:S(2)}) collective-permute-start(bf16[512,384]{1,0:T(8,128)(2,1)S(1)} %collective-permute-done.4.refs_3_), channel_id=1, source_target_pairs={{0,64},{64,0},{1,65},{65,1},{2,66},{66,2},{3,67},{67,3},{4,68},{68... | collective-permute-start | bytes 1179656 | tf_op jit(solution)/shard_map/ppermute | solution.py:287
  81.3 3.8 %collective-permute-start.11 = (bf16[512,384]{1,0:T(8,128)(2,1)S(1)}, bf16[512,384]{1,0:T(8,128)(2,1)}, u32[]{:S(2)}, u32[]{:S(2)}) collective-permute-start(bf16[512,384]{1,0:T(8,128)(2,1)S(1)} %collective-permute-done.5.refs_4_), channel_id=1, source_target_pairs={{0,64},{64,0},{1,65},{65,1},{2,66},{66,2},{3,67},{67,3},{4,68},{68... | collective-permute-start | bytes 1179656 | tf_op jit(solution)/shard_map/ppermute | solution.py:287
  85.1 0.7 copy.17
  85.8 15.2 %all-to-all-start = ((f32[16,16,128]{2,1,0:T(8,128)}), f32[16,16,128]{2,1,0:T(8,128)S(1)}, u32[]{:S(2)}, u32[]{:S(2)}) async-start(f32[16,16,128]{2,1,0:T(8,128)} %slice_add_fusion), calls=%async_computation | async-start | bytes 262144 | tf_op jit(solution)/shard_map/all_to_all | solution.py:289
  101.0 0.0 collective-permute-done.10.refs_8_
  101.0 0.0 collective-permute-done.8.refs_6_
  101.0 0.0 collective-permute-done.9.refs_7_
  101.0 0.0 all-gather.3.cloned.1.call-done
  101.1 7.5 %shard_map.102 = (bf16[256,384]{1,0:T(8,128)(2,1)}, bf16[256,384]{1,0:T(8,128)(2,1)}) custom-call(s32[1]{0:T(128)} %bitcast.1.first_ref, bf16[16,2,16,8192]{3,2,1,0:T(8,128)(2,1)} %bitcast.43, bf16[1024,384]{1,0:T(8,128)(2,1)} %copy-done.10, bf16[1024,384]{1,0:T(8,128)(2,1)} %copy-done.8, bf16[1024,384]{1,0:T(8,128)(2,1)} %copy-done.9, ...), custom_call_target="tpu_custom_call" | custom-call | flops 3221225472 | bytes 14680064 | tf_op jit(solution)/shard_map/pallas_call | solution.py:96
  108.6 1.6 %collective-permute-start.12 = (bf16[256,384]{1,0:T(8,128)(2,1)}, bf16[256,384]{1,0:T(8,128)(2,1)S(1)}, u32[]{:S(2)}, u32[]{:S(2)}) collective-permute-start(bf16[256,384]{1,0:T(8,128)(2,1)} %get-tuple-element.22), channel_id=1, source_target_pairs={{0,0},{16,32},{32,16},{48,48},{1,1},{17,33},{33,17},{49,49},{2,2},... | collective-permute-start | bytes 589832 | tf_op jit(solution)/shard_map/ppermute | solution.py:272
  110.2 2.6 %collective-permute-start.13 = (bf16[256,384]{1,0:T(8,128)(2,1)}, bf16[256,384]{1,0:T(8,128)(2,1)S(1)}, u32[]{:S(2)}, u32[]{:S(2)}) collective-permute-start(bf16[256,384]{1,0:T(8,128)(2,1)} %get-tuple-element.23), channel_id=1, source_target_pairs={{0,32},{16,0},{32,48},{48,16},{1,33},{17,1},{33,49},{49,17},{2,34}... | collective-permute-start | bytes 589832 | tf_op jit(solution)/shard_map/ppermute | solution.py:272
  112.8 0.7 dynamic-slice_bitcast_fusion.rates_ref
  113.5 0.2 all-to-all-done.partial_ref
  113.7 5.8 %collective-permute-done.13.other_ref = bf16[256,384]{1,0:T(8,128)(2,1)S(1)} collective-permute-done((bf16[256,384]{1,0:T(8,128)(2,1)}, bf16[256,384]{1,0:T(8,128)(2,1)S(1)}, u32[]{:S(2)}, u32[]{:S(2)}) %collective-permute-start.13) | collective-permute-done | bytes 196640 | tf_op jit(solution)/shard_map/ppermute | solution.py:272
  119.5 2.6 %shard_map.103 = bf16[512,128]{1,0:T(8,128)(2,1)} custom-call(s32[1]{0:T(128)} %bitcast.half_ref, bf16[256,384]{1,0:T(8,128)(2,1)S(1)} %collective-permute-done.12.mine_ref, bf16[256,384]{1,0:T(8,128)(2,1)S(1)} %collective-permute-done.13.other_ref, f32[8,384]{1,0:T(8,128)S(1)} %pad_convert_fusion.tail_ref, f32[7,384]{1,0:T(8,128)S(1)} %bitcast.40, ...), custom_call_target="tpu_custom_call" | custom-call | flops 11796480 | bytes 524288 | tf_op jit(solution)/shard_map/pallas_call | solution.py:221
  (28 shorter events, 0.2 us)
Async XLA Ops:
  6.5 94.5 %all-gather.3.cloned.1.call-start = ((), (), s32[]{:S(2)}) async-start(), calls=%async_computation.1 | async-start | bytes 8650752 | tf_op jit(solution)/shard_map/all_gather | solution.py:266
  6.6 1.0 copy-start.2
  7.6 0.8 copy-start.3
  11.2 6.9 %collective-permute-start = (bf16[512,384]{1,0:T(8,128)(2,1)S(1)}, bf16[512,384]{1,0:T(8,128)(2,1)S(1)}, u32[]{:S(2)}, u32[]{:S(2)}) collective-permute-start(bf16[512,384]{1,0:T(8,128)(2,1)S(1)} %copy.13), channel_id=1, source_target_pairs={{0,0},{16,32},{32,16},{48,48},{1,1},{17,33},{33,17},{49,49},{2,2},... | collective-permute-start | bytes 1179656 | tf_op jit(solution)/shard_map/ppermute | solution.py:272
  11.9 13.2 %collective-permute-start.1 = (bf16[512,384]{1,0:T(8,128)(2,1)S(1)}, bf16[512,384]{1,0:T(8,128)(2,1)S(1)}, u32[]{:S(2)}, u32[]{:S(2)}) collective-permute-start(bf16[512,384]{1,0:T(8,128)(2,1)S(1)} %copy.13), channel_id=1, source_target_pairs={{0,16},{16,48},{32,0},{48,32},{1,17},{17,49},{33,1},{49,33},{2,18}... | collective-permute-start | bytes 1179656 | tf_op jit(solution)/shard_map/ppermute | solution.py:272
  25.1 75.9 %copy-start.10 = (bf16[1024,384]{1,0:T(8,128)(2,1)}, bf16[1024,384]{1,0:T(8,128)(2,1)S(1)}, u32[]{:S(2)}) copy-start(bf16[1024,384]{1,0:T(8,128)(2,1)S(1)} %constant_dynamic-update-slice_fusion.refs_0_) | copy-start | bytes 2359300
  25.1 23.2 %collective-permute-start.2 = (bf16[1024,384]{1,0:T(8,128)(2,1)S(1)}, bf16[1024,384]{1,0:T(8,128)(2,1)S(1)}, u32[]{:S(2)}, u32[]{:S(2)}) collective-permute-start(bf16[1024,384]{1,0:T(8,128)(2,1)S(1)} %constant_dynamic-update-slice_fusion.refs_0_), channel_id=1, source_target_pairs={{0,128},{128,256},{256,384},{384,0},{1,129},{129,257},{257,385},{3... | collective-permute-start | bytes 2359304 | tf_op jit(solution)/shard_map/ppermute | solution.py:242
  28.6 22.3 %collective-permute-start.3 = (bf16[1024,384]{1,0:T(8,128)(2,1)S(1)}, bf16[1024,384]{1,0:T(8,128)(2,1)S(1)}, u32[]{:S(2)}, u32[]{:S(2)}) collective-permute-start(bf16[1024,384]{1,0:T(8,128)(2,1)S(1)} %constant_dynamic-update-slice_fusion.refs_0_), channel_id=1, source_target_pairs={{0,384},{128,0},{256,128},{384,256},{1,385},{129,1},{257,129},{385... | collective-permute-start | bytes 2359304 | tf_op jit(solution)/shard_map/ppermute | solution.py:243
  32.2 30.9 %collective-permute-start.6 = (bf16[1024,384]{1,0:T(8,128)(2,1)S(1)}, bf16[1024,384]{1,0:T(8,128)(2,1)}, u32[]{:S(2)}, u32[]{:S(2)}) collective-permute-start(bf16[1024,384]{1,0:T(8,128)(2,1)S(1)} %constant_dynamic-update-slice_fusion.refs_0_), channel_id=1, source_target_pairs={{0,64},{64,0},{1,65},{65,1},{2,66},{66,2},{3,67},{67,3},{4,68},{68... | collective-permute-start | bytes 2359304 | tf_op jit(solution)/shard_map/ppermute | solution.py:276
  48.3 52.7 %copy-start.8 = (bf16[1024,384]{1,0:T(8,128)(2,1)}, bf16[1024,384]{1,0:T(8,128)(2,1)S(1)}, u32[]{:S(2)}) copy-start(bf16[1024,384]{1,0:T(8,128)(2,1)S(1)} %collective-permute-done.2.refs_1_) | copy-start | bytes 2359300
  48.3 30.8 %collective-permute-start.4 = (bf16[512,384]{1,0:T(8,128)(2,1)S(1)}, bf16[512,384]{1,0:T(8,128)(2,1)S(1)}, u32[]{:S(2)}, u32[]{:S(2)}) collective-permute-start(bf16[512,384]{1,0:T(8,128)(2,1)S(1)} %slice.16), channel_id=1, source_target_pairs={{0,128},{128,256},{256,384},{384,0},{1,129},{129,257},{257,385},{3... | collective-permute-start | bytes 1179656 | tf_op jit(solution)/shard_map/ppermute | solution.py:238
  50.9 50.2 %copy-start.9 = (bf16[1024,384]{1,0:T(8,128)(2,1)}, bf16[1024,384]{1,0:T(8,128)(2,1)S(1)}, u32[]{:S(2)}) copy-start(bf16[1024,384]{1,0:T(8,128)(2,1)S(1)} %collective-permute-done.3.refs_2_) | copy-start | bytes 2359300
  50.9 28.2 %collective-permute-start.5 = (bf16[512,384]{1,0:T(8,128)(2,1)S(1)}, bf16[512,384]{1,0:T(8,128)(2,1)S(1)}, u32[]{:S(2)}, u32[]{:S(2)}) collective-permute-start(bf16[512,384]{1,0:T(8,128)(2,1)S(1)} %slice.17), channel_id=1, source_target_pairs={{0,384},{128,0},{256,128},{384,256},{1,385},{129,1},{257,129},{385... | collective-permute-start | bytes 1179656 | tf_op jit(solution)/shard_map/ppermute | solution.py:238
  55.7 1.3 copy-start
  57.0 1.0 copy-start.1
  57.9 0.7 copy-start.6
  58.6 60.9 %copy-start.4 = (f32[7,3,128]{2,0,1:T(8,128)S(1)}, f32[7,3,128]{2,0,1:T(8,128)}, u32[]{:S(2)}) copy-start(f32[7,3,128]{2,0,1:T(8,128)} %param.14) | copy-start | bytes 32260
  58.6 60.9 %copy-start.5 = (f32[128,16]{0,1:T(8,128)S(1)}, f32[128,16]{0,1:T(8,128)}, u32[]{:S(2)}) copy-start(f32[128,16]{0,1:T(8,128)} %param.16) | copy-start | bytes 24580
  58.6 60.9 %copy-start.7 = (f32[128]{0:T(128)S(1)}, f32[128]{0:T(128)}, u32[]{:S(2)}) copy-start(f32[128]{0:T(128)} %param.17) | copy-start | bytes 1540
  63.0 37.9 %collective-permute-start.8 = (bf16[1024,384]{1,0:T(8,128)(2,1)}, bf16[1024,384]{1,0:T(8,128)(2,1)}, u32[]{:S(2)}, u32[]{:S(2)}) collective-permute-start(bf16[1024,384]{1,0:T(8,128)(2,1)} %collective-permute-done.6.refs_5_), channel_id=1, source_target_pairs={{0,128},{128,256},{256,384},{384,0},{1,129},{129,257},{257,385},{3... | collective-permute-start | bytes 2359304 | tf_op jit(solution)/shard_map/ppermute | solution.py:285
  65.0 36.0 %collective-permute-start.9 = (bf16[1024,384]{1,0:T(8,128)(2,1)}, bf16[1024,384]{1,0:T(8,128)(2,1)}, u32[]{:S(2)}, u32[]{:S(2)}) collective-permute-start(bf16[1024,384]{1,0:T(8,128)(2,1)} %collective-permute-done.6.refs_5_), channel_id=1, source_target_pairs={{0,384},{128,0},{256,128},{384,256},{1,385},{129,1},{257,129},{385... | collective-permute-start | bytes 2359304 | tf_op jit(solution)/shard_map/ppermute | solution.py:285
  70.1 8.4 %collective-permute-start.7 = (f32[16,16,128]{2,1,0:T(8,128)S(1)}, f32[16,16,128]{2,1,0:T(8,128)S(1)}, u32[]{:S(2)}, u32[]{:S(2)}) collective-permute-start(f32[16,16,128]{2,1,0:T(8,128)S(1)} %slice.15), channel_id=1, source_target_pairs={{0,16},{16,0},{1,17},{17,1},{2,18},{18,2},{3,19},{19,3},{4,20},{20... | collective-permute-start | bytes 393224 | tf_op jit(solution)/shard_map/ppermute | solution.py:284
  79.2 21.9 %copy-start.11 = (bf16[512,384]{1,0:T(8,128)(2,1)}, bf16[512,384]{1,0:T(8,128)(2,1)S(1)}, u32[]{:S(2)}) copy-start(bf16[512,384]{1,0:T(8,128)(2,1)S(1)} %collective-permute-done.4.refs_3_) | copy-start | bytes 1179652
  79.2 21.9 %copy-start.12 = (bf16[512,384]{1,0:T(8,128)(2,1)}, bf16[512,384]{1,0:T(8,128)(2,1)S(1)}, u32[]{:S(2)}) copy-start(bf16[512,384]{1,0:T(8,128)(2,1)S(1)} %collective-permute-done.5.refs_4_) | copy-start | bytes 1179652
  79.2 21.8 %collective-permute-start.10 = (bf16[512,384]{1,0:T(8,128)(2,1)S(1)}, bf16[512,384]{1,0:T(8,128)(2,1)}, u32[]{:S(2)}, u32[]{:S(2)}) collective-permute-start(bf16[512,384]{1,0:T(8,128)(2,1)S(1)} %collective-permute-done.4.refs_3_), channel_id=1, source_target_pairs={{0,64},{64,0},{1,65},{65,1},{2,66},{66,2},{3,67},{67,3},{4,68},{68... | collective-permute-start | bytes 1179656 | tf_op jit(solution)/shard_map/ppermute | solution.py:287
  81.3 19.7 %collective-permute-start.11 = (bf16[512,384]{1,0:T(8,128)(2,1)S(1)}, bf16[512,384]{1,0:T(8,128)(2,1)}, u32[]{:S(2)}, u32[]{:S(2)}) collective-permute-start(bf16[512,384]{1,0:T(8,128)(2,1)S(1)} %collective-permute-done.5.refs_4_), channel_id=1, source_target_pairs={{0,64},{64,0},{1,65},{65,1},{2,66},{66,2},{3,67},{67,3},{4,68},{68... | collective-permute-start | bytes 1179656 | tf_op jit(solution)/shard_map/ppermute | solution.py:287
  85.8 27.9 %all-to-all-start = ((f32[16,16,128]{2,1,0:T(8,128)}), f32[16,16,128]{2,1,0:T(8,128)S(1)}, u32[]{:S(2)}, u32[]{:S(2)}) async-start(f32[16,16,128]{2,1,0:T(8,128)} %slice_add_fusion), calls=%async_computation | async-start | bytes 262144 | tf_op jit(solution)/shard_map/all_to_all | solution.py:289
  108.6 5.1 %collective-permute-start.12 = (bf16[256,384]{1,0:T(8,128)(2,1)}, bf16[256,384]{1,0:T(8,128)(2,1)S(1)}, u32[]{:S(2)}, u32[]{:S(2)}) collective-permute-start(bf16[256,384]{1,0:T(8,128)(2,1)} %get-tuple-element.22), channel_id=1, source_target_pairs={{0,0},{16,32},{32,16},{48,48},{1,1},{17,33},{33,17},{49,49},{2,2},... | collective-permute-start | bytes 589832 | tf_op jit(solution)/shard_map/ppermute | solution.py:272
  110.2 9.3 %collective-permute-start.13 = (bf16[256,384]{1,0:T(8,128)(2,1)}, bf16[256,384]{1,0:T(8,128)(2,1)S(1)}, u32[]{:S(2)}, u32[]{:S(2)}) collective-permute-start(bf16[256,384]{1,0:T(8,128)(2,1)} %get-tuple-element.23), channel_id=1, source_target_pairs={{0,32},{16,0},{32,48},{48,16},{1,33},{17,1},{33,49},{49,17},{2,34}... | collective-permute-start | bytes 589832 | tf_op jit(solution)/shard_map/ppermute | solution.py:272
Sparse Core Ops, SparseCore 0:
  9.9 83.4 all-gather.2

commit v5 on v4

--- a/solution.py
+++ b/solution.py
@@ -279,8 +279,9 @@
     behind = (seq_count - 1 - seq_index) * ctx_rows
     where = jnp.stack([xh, behind]).astype(jnp.int32)
     sums = context_sums(context_u[0], context_tokens, rates_t, where, chans)
-    far, sums = lax.optimization_barrier((far, sums))
-    near_pieces = ring_gather(near, "y", y_count)
+    near_before, near_after = (step("y", y_count, by)(near) for by in (1, -1))
+    near_before, near_after, far, sums = lax.optimization_barrier((near_before, near_after, far, sums))
+    near_pieces = (near, near_before, near_after) + ring_ends(near_before, near_after, "y", y_count)
     sums = sums[:z_count] + step("xh", 2, 1)(sums[z_count:])
     before, after = (step("y", y_count, by)(far) for by in (1, -1))
     *near_pieces, low, high, sums = lax.optimization_barrier((*near_pieces, sums))

time: 130 us -> 128 us (0.985)
    ppermute x2, waiting for transfers between devices: 13.7 us -> 8.83 us  [local(): near_before, near_after = (step('y', y_count, by)(near) for by in (1, -1))]
    ppermute x1, waiting for transfers between devices: 0.01 us -> 3.47 us  [local(): far = step('xl', 2, 1)(near)]
  transfers between devices with their start and end apart: 16 -> 16, of which waited for: 6 -> 7; matrix products, arithmetic and copies ran while one was open for 3% -> 3% of each run, Pallas kernels for 9% -> 9%
where the time goes in v5:
time: 128 us
  starting transfers between devices  57.6 us (45%)
  waiting for transfers between devices  31.9 us (25%)
  Pallas kernels  16 us (12%)
  between operations  13.7 us (11%)
  local copies, waits for them, and re-layouts  7.64 us (6%)
    all_to_all x1, starting transfers between devices, local(): partial = lax.all_to_all(sums, 'z', split_axis=0, concat_axis=0, tiled=True)  15.2 us
    ppermute x4, waiting for transfers between devices, swap(): return lax.ppermute(block, ('core', 'xh'), pairs)  12.9 us
    ppermute x4, starting transfers between devices, swap(): return lax.ppermute(block, ('core', 'xh'), pairs)  10.8 us
    ppermute x2, waiting for transfers between devices, local(): near_before, near_after = (step('y', y_count, by)(near) for by in (1, -1))  8.83 us
    pallas_call x1, Pallas kernels, project(): pl.pallas_call(project_kernel, out_shape=(shape, shape), in_specs=[pl.Blo...  7.51 us
    ppermute x2, starting transfers between devices, local(): before, after = (step('y', y_count, by)(far) for by in (1, -1))  7.06 us
    ppermute x2, starting transfers between devices, local(): near_before, near_after = (step('y', y_count, by)(near) for by in (1, -1))  7.05 us
    unnamed x29, local copies, waits for them, and re-layouts  6.48 us
  transfers between devices with their start and end apart: 16, of which 7 were waited for; matrix products, arithmetic and copies ran while one was open for 3% of the time, Pallas kernels for 9%

profile of v5, /device:TPU:32, one launch (start us, length us, event | category | flops | bytes accessed | tf_op | source)
XLA Modules:
  0.0 127.6 jit_solution(17279478451370750716)
XLA Ops:
  6.5 0.1 stack.74.order_ref
  6.6 0.0 copy-start.2
  6.6 0.9 copy-done.2
  7.6 0.8 copy-done.3
  8.3 1.4 %shard_map.100 = bf16[16,8192]{1,0:T(8,128)(2,1)} custom-call(bf16[16,8192]{1,0:T(8,128)(2,1)S(1)} %bitcast.38, f32[1,8192]{1,0:T(1,128)S(1)} %bitcast.39, s32[16]{0:T(128)S(1)} %stack.74.order_ref), custom_call_target="tpu_custom_call" | custom-call | flops 1048576 | bytes 524288 | tf_op jit(solution)/shard_map/pallas_call | solution.py:40
  9.8 0.0 all-gather.3.cloned.1.call-update
  9.8 1.2 copy.12
  11.0 0.2 copy.13
  11.2 0.7 collective-permute-start
  11.9 6.2 %collective-permute-start.1 = (bf16[512,384]{1,0:T(8,128)(2,1)S(1)}, bf16[512,384]{1,0:T(8,128)(2,1)S(1)}, u32[]{:S(2)}, u32[]{:S(2)}) collective-permute-start(bf16[512,384]{1,0:T(8,128)(2,1)S(1)} %copy.13), channel_id=1, source_target_pairs={{0,16},{16,48},{32,0},{48,32},{1,17},{17,49},{33,1},{49,33},{2,18}... | collective-permute-start | bytes 1179656 | tf_op jit(solution)/shard_map/ppermute | solution.py:272
  18.1 0.0 collective-permute-done
  18.1 6.9 %collective-permute-done.1 = bf16[512,384]{1,0:T(8,128)(2,1)S(1)} collective-permute-done((bf16[512,384]{1,0:T(8,128)(2,1)S(1)}, bf16[512,384]{1,0:T(8,128)(2,1)S(1)}, u32[]{:S(2)}, u32[]{:S(2)}) %collective-permute-start.1) | collective-permute-done | bytes 393248 | tf_op jit(solution)/shard_map/ppermute | solution.py:272
  25.0 0.1 constant_dynamic-update-slice_fusion.refs_0_
  25.1 3.5 %collective-permute-start.2 = (bf16[1024,384]{1,0:T(8,128)(2,1)S(1)}, bf16[1024,384]{1,0:T(8,128)(2,1)S(1)}, u32[]{:S(2)}, u32[]{:S(2)}) collective-permute-start(bf16[1024,384]{1,0:T(8,128)(2,1)S(1)} %constant_dynamic-update-slice_fusion.refs_0_), channel_id=1, source_target_pairs={{0,128},{128,256},{256,384},{384,0},{1,129},{129,257},{257,385},{3... | collective-permute-start | bytes 2359304 | tf_op jit(solution)/shard_map/ppermute | solution.py:282
  28.6 3.6 %collective-permute-start.3 = (bf16[1024,384]{1,0:T(8,128)(2,1)S(1)}, bf16[1024,384]{1,0:T(8,128)(2,1)S(1)}, u32[]{:S(2)}, u32[]{:S(2)}) collective-permute-start(bf16[1024,384]{1,0:T(8,128)(2,1)S(1)} %constant_dynamic-update-slice_fusion.refs_0_), channel_id=1, source_target_pairs={{0,384},{128,0},{256,128},{384,256},{1,385},{129,1},{257,129},{385... | collective-permute-start | bytes 2359304 | tf_op jit(solution)/shard_map/ppermute | solution.py:282
  32.2 2.5 %collective-permute-start.4 = (bf16[1024,384]{1,0:T(8,128)(2,1)S(1)}, bf16[1024,384]{1,0:T(8,128)(2,1)}, u32[]{:S(2)}, u32[]{:S(2)}) collective-permute-start(bf16[1024,384]{1,0:T(8,128)(2,1)S(1)} %constant_dynamic-update-slice_fusion.refs_0_), channel_id=1, source_target_pairs={{0,64},{64,0},{1,65},{65,1},{2,66},{66,2},{3,67},{67,3},{4,68},{68... | collective-permute-start | bytes 2359304 | tf_op jit(solution)/shard_map/ppermute | solution.py:276
  34.7 0.1 pad_add_fusion.where_ref
  34.8 1.2 copy-done
  36.0 0.9 copy-done.1
  37.0 0.7 copy-done.6
  37.6 4.4 %shard_map.101 = f32[32,16,128]{2,1,0:T(8,128)S(1)} custom-call(s32[2]{0:T(128)S(1)} %pad_add_fusion.where_ref, bf16[128,4096]{1,0:T(8,128)(2,1)S(1)} %bitcast.36, s32[1,128]{1,0:T(1,128)S(1)} %copy-done.6, f32[16,4096]{1,0:T(8,128)S(1)} %bitcast.37), custom_call_target="tpu_custom_call" | custom-call | flops 16777216 | bytes 1048576 | tf_op jit(solution)/shard_map/pallas_call | solution.py:153
  42.1 6.2 %collective-permute-done.2.refs_1_ = bf16[1024,384]{1,0:T(8,128)(2,1)S(1)} collective-permute-done((bf16[1024,384]{1,0:T(8,128)(2,1)S(1)}, bf16[1024,384]{1,0:T(8,128)(2,1)S(1)}, u32[]{:S(2)}, u32[]{:S(2)}) %collective-permute-start.2) | collective-permute-done | bytes 786464 | tf_op jit(solution)/shard_map/ppermute | solution.py:282
  48.3 2.6 %collective-permute-done.3.refs_2_ = bf16[1024,384]{1,0:T(8,128)(2,1)S(1)} collective-permute-done((bf16[1024,384]{1,0:T(8,128)(2,1)S(1)}, bf16[1024,384]{1,0:T(8,128)(2,1)S(1)}, u32[]{:S(2)}, u32[]{:S(2)}) %collective-permute-start.3) | collective-permute-done | bytes 786464 | tf_op jit(solution)/shard_map/ppermute | solution.py:282
  50.9 3.5 %collective-permute-done.4.refs_5_ = bf16[1024,384]{1,0:T(8,128)(2,1)} collective-permute-done((bf16[1024,384]{1,0:T(8,128)(2,1)S(1)}, bf16[1024,384]{1,0:T(8,128)(2,1)}, u32[]{:S(2)}, u32[]{:S(2)}) %collective-permute-start.4) | collective-permute-done | bytes 786464 | tf_op jit(solution)/shard_map/ppermute | solution.py:276
  54.4 0.0 copy-start.4
  54.4 0.0 copy-start.5
  54.4 0.0 copy-start.7
  54.4 2.3 %collective-permute-start.5 = (bf16[512,384]{1,0:T(8,128)(2,1)S(1)}, bf16[512,384]{1,0:T(8,128)(2,1)S(1)}, u32[]{:S(2)}, u32[]{:S(2)}) collective-permute-start(bf16[512,384]{1,0:T(8,128)(2,1)S(1)} %slice.12), channel_id=1, source_target_pairs={{0,128},{128,256},{256,384},{384,0},{1,129},{129,257},{257,385},{3... | collective-permute-start | bytes 1179656 | tf_op jit(solution)/shard_map/ppermute | solution.py:238
  56.8 4.8 %collective-permute-start.6 = (bf16[512,384]{1,0:T(8,128)(2,1)S(1)}, bf16[512,384]{1,0:T(8,128)(2,1)S(1)}, u32[]{:S(2)}, u32[]{:S(2)}) collective-permute-start(bf16[512,384]{1,0:T(8,128)(2,1)S(1)} %slice.13), channel_id=1, source_target_pairs={{0,384},{128,0},{256,128},{384,256},{1,385},{129,1},{257,129},{385... | collective-permute-start | bytes 1179656 | tf_op jit(solution)/shard_map/ppermute | solution.py:238
  61.7 1.9 %collective-permute-start.8 = (bf16[1024,384]{1,0:T(8,128)(2,1)}, bf16[1024,384]{1,0:T(8,128)(2,1)}, u32[]{:S(2)}, u32[]{:S(2)}) collective-permute-start(bf16[1024,384]{1,0:T(8,128)(2,1)} %collective-permute-done.4.refs_5_), channel_id=1, source_target_pairs={{0,128},{128,256},{256,384},{384,0},{1,129},{129,257},{257,385},{3... | collective-permute-start | bytes 2359304 | tf_op jit(solution)/shard_map/ppermute | solution.py:286
  63.6 5.1 %collective-permute-start.9 = (bf16[1024,384]{1,0:T(8,128)(2,1)}, bf16[1024,384]{1,0:T(8,128)(2,1)}, u32[]{:S(2)}, u32[]{:S(2)}) collective-permute-start(bf16[1024,384]{1,0:T(8,128)(2,1)} %collective-permute-done.4.refs_5_), channel_id=1, source_target_pairs={{0,384},{128,0},{256,128},{384,256},{1,385},{129,1},{257,129},{385... | collective-permute-start | bytes 2359304 | tf_op jit(solution)/shard_map/ppermute | solution.py:286
  68.8 1.9 %collective-permute-start.7 = (f32[16,16,128]{2,1,0:T(8,128)S(1)}, f32[16,16,128]{2,1,0:T(8,128)S(1)}, u32[]{:S(2)}, u32[]{:S(2)}) collective-permute-start(f32[16,16,128]{2,1,0:T(8,128)S(1)} %slice.15), channel_id=1, source_target_pairs={{0,16},{16,0},{1,17},{17,1},{2,18},{18,2},{3,19},{19,3},{4,20},{20... | collective-permute-start | bytes 393224 | tf_op jit(solution)/shard_map/ppermute | solution.py:285
  70.7 6.4 %collective-permute-done.7 = f32[16,16,128]{2,1,0:T(8,128)S(1)} collective-permute-done((f32[16,16,128]{2,1,0:T(8,128)S(1)}, f32[16,16,128]{2,1,0:T(8,128)S(1)}, u32[]{:S(2)}, u32[]{:S(2)}) %collective-permute-start.7) | collective-permute-done | bytes 131104 | tf_op jit(solution)/shard_map/ppermute | solution.py:285
  77.1 0.7 slice_add_fusion
  77.8 2.5 %collective-permute-start.10 = (bf16[512,384]{1,0:T(8,128)(2,1)S(1)}, bf16[512,384]{1,0:T(8,128)(2,1)}, u32[]{:S(2)}, u32[]{:S(2)}) collective-permute-start(bf16[512,384]{1,0:T(8,128)(2,1)S(1)} %collective-permute-done.5.refs_3_), channel_id=1, source_target_pairs={{0,64},{64,0},{1,65},{65,1},{2,66},{66,2},{3,67},{67,3},{4,68},{68... | collective-permute-start | bytes 1179656 | tf_op jit(solution)/shard_map/ppermute | solution.py:288
  80.3 3.4 %collective-permute-start.11 = (bf16[512,384]{1,0:T(8,128)(2,1)S(1)}, bf16[512,384]{1,0:T(8,128)(2,1)}, u32[]{:S(2)}, u32[]{:S(2)}) collective-permute-start(bf16[512,384]{1,0:T(8,128)(2,1)S(1)} %collective-permute-done.6.refs_4_), channel_id=1, source_target_pairs={{0,64},{64,0},{1,65},{65,1},{2,66},{66,2},{3,67},{67,3},{4,68},{68... | collective-permute-start | bytes 1179656 | tf_op jit(solution)/shard_map/ppermute | solution.py:288
  83.7 0.7 copy.17
  84.4 15.2 %all-to-all-start = ((f32[16,16,128]{2,1,0:T(8,128)}), f32[16,16,128]{2,1,0:T(8,128)S(1)}, u32[]{:S(2)}, u32[]{:S(2)}) async-start(f32[16,16,128]{2,1,0:T(8,128)} %slice_add_fusion), calls=%async_computation | async-start | bytes 262144 | tf_op jit(solution)/shard_map/all_to_all | solution.py:290
  99.6 0.0 collective-permute-done.11.refs_9_
  99.6 0.0 collective-permute-done.9.refs_7_
  99.7 0.0 all-gather.3.cloned.1.call-done
  99.7 7.5 %shard_map.102 = (bf16[256,384]{1,0:T(8,128)(2,1)}, bf16[256,384]{1,0:T(8,128)(2,1)}) custom-call(s32[1]{0:T(128)} %bitcast.1.first_ref, bf16[16,2,16,8192]{3,2,1,0:T(8,128)(2,1)} %bitcast.43, bf16[1024,384]{1,0:T(8,128)(2,1)} %copy-done.10, bf16[1024,384]{1,0:T(8,128)(2,1)} %copy-done.8, bf16[1024,384]{1,0:T(8,128)(2,1)} %copy-done.9, ...), custom_call_target="tpu_custom_call" | custom-call | flops 3221225472 | bytes 14680064 | tf_op jit(solution)/shard_map/pallas_call | solution.py:96
  107.3 1.6 %collective-permute-start.12 = (bf16[256,384]{1,0:T(8,128)(2,1)}, bf16[256,384]{1,0:T(8,128)(2,1)S(1)}, u32[]{:S(2)}, u32[]{:S(2)}) collective-permute-start(bf16[256,384]{1,0:T(8,128)(2,1)} %get-tuple-element.26), channel_id=1, source_target_pairs={{0,0},{16,32},{32,16},{48,48},{1,1},{17,33},{33,17},{49,49},{2,2},... | collective-permute-start | bytes 589832 | tf_op jit(solution)/shard_map/ppermute | solution.py:272
  108.8 2.4 %collective-permute-start.13 = (bf16[256,384]{1,0:T(8,128)(2,1)}, bf16[256,384]{1,0:T(8,128)(2,1)S(1)}, u32[]{:S(2)}, u32[]{:S(2)}) collective-permute-start(bf16[256,384]{1,0:T(8,128)(2,1)} %get-tuple-element.27), channel_id=1, source_target_pairs={{0,32},{16,0},{32,48},{48,16},{1,33},{17,1},{33,49},{49,17},{2,34}... | collective-permute-start | bytes 589832 | tf_op jit(solution)/shard_map/ppermute | solution.py:272
  111.2 0.7 dynamic-slice_bitcast_fusion.rates_ref
  111.9 0.2 all-to-all-done.partial_ref
  112.1 6.0 %collective-permute-done.13.other_ref = bf16[256,384]{1,0:T(8,128)(2,1)S(1)} collective-permute-done((bf16[256,384]{1,0:T(8,128)(2,1)}, bf16[256,384]{1,0:T(8,128)(2,1)S(1)}, u32[]{:S(2)}, u32[]{:S(2)}) %collective-permute-start.13) | collective-permute-done | bytes 196640 | tf_op jit(solution)/shard_map/ppermute | solution.py:272
  118.1 2.6 %shard_map.103 = bf16[512,128]{1,0:T(8,128)(2,1)} custom-call(s32[1]{0:T(128)} %bitcast.half_ref, bf16[256,384]{1,0:T(8,128)(2,1)S(1)} %collective-permute-done.12.mine_ref, bf16[256,384]{1,0:T(8,128)(2,1)S(1)} %collective-permute-done.13.other_ref, f32[8,384]{1,0:T(8,128)S(1)} %pad_convert_fusion.tail_ref, f32[7,384]{1,0:T(8,128)S(1)} %bitcast.40, ...), custom_call_target="tpu_custom_call" | custom-call | flops 11796480 | bytes 524288 | tf_op jit(solution)/shard_map/pallas_call | solution.py:221
  (28 shorter events, 0.2 us)
Async XLA Ops:
  6.5 93.1 %all-gather.3.cloned.1.call-start = ((), (), s32[]{:S(2)}) async-start(), calls=%async_computation.1 | async-start | bytes 8650752 | tf_op jit(solution)/shard_map/all_gather | solution.py:266
  6.6 1.0 copy-start.2
  7.6 0.8 copy-start.3
  11.2 6.9 %collective-permute-start = (bf16[512,384]{1,0:T(8,128)(2,1)S(1)}, bf16[512,384]{1,0:T(8,128)(2,1)S(1)}, u32[]{:S(2)}, u32[]{:S(2)}) collective-permute-start(bf16[512,384]{1,0:T(8,128)(2,1)S(1)} %copy.13), channel_id=1, source_target_pairs={{0,0},{16,32},{32,16},{48,48},{1,1},{17,33},{33,17},{49,49},{2,2},... | collective-permute-start | bytes 1179656 | tf_op jit(solution)/shard_map/ppermute | solution.py:272
  11.9 13.2 %collective-permute-start.1 = (bf16[512,384]{1,0:T(8,128)(2,1)S(1)}, bf16[512,384]{1,0:T(8,128)(2,1)S(1)}, u32[]{:S(2)}, u32[]{:S(2)}) collective-permute-start(bf16[512,384]{1,0:T(8,128)(2,1)S(1)} %copy.13), channel_id=1, source_target_pairs={{0,16},{16,48},{32,0},{48,32},{1,17},{17,49},{33,1},{49,33},{2,18}... | collective-permute-start | bytes 1179656 | tf_op jit(solution)/shard_map/ppermute | solution.py:272
  25.1 74.6 %copy-start.10 = (bf16[1024,384]{1,0:T(8,128)(2,1)}, bf16[1024,384]{1,0:T(8,128)(2,1)S(1)}, u32[]{:S(2)}) copy-start(bf16[1024,384]{1,0:T(8,128)(2,1)S(1)} %constant_dynamic-update-slice_fusion.refs_0_) | copy-start | bytes 2359300
  25.1 23.2 %collective-permute-start.2 = (bf16[1024,384]{1,0:T(8,128)(2,1)S(1)}, bf16[1024,384]{1,0:T(8,128)(2,1)S(1)}, u32[]{:S(2)}, u32[]{:S(2)}) collective-permute-start(bf16[1024,384]{1,0:T(8,128)(2,1)S(1)} %constant_dynamic-update-slice_fusion.refs_0_), channel_id=1, source_target_pairs={{0,128},{128,256},{256,384},{384,0},{1,129},{129,257},{257,385},{3... | collective-permute-start | bytes 2359304 | tf_op jit(solution)/shard_map/ppermute | solution.py:282
  28.6 22.3 %collective-permute-start.3 = (bf16[1024,384]{1,0:T(8,128)(2,1)S(1)}, bf16[1024,384]{1,0:T(8,128)(2,1)S(1)}, u32[]{:S(2)}, u32[]{:S(2)}) collective-permute-start(bf16[1024,384]{1,0:T(8,128)(2,1)S(1)} %constant_dynamic-update-slice_fusion.refs_0_), channel_id=1, source_target_pairs={{0,384},{128,0},{256,128},{384,256},{1,385},{129,1},{257,129},{385... | collective-permute-start | bytes 2359304 | tf_op jit(solution)/shard_map/ppermute | solution.py:282
  32.2 22.2 %collective-permute-start.4 = (bf16[1024,384]{1,0:T(8,128)(2,1)S(1)}, bf16[1024,384]{1,0:T(8,128)(2,1)}, u32[]{:S(2)}, u32[]{:S(2)}) collective-permute-start(bf16[1024,384]{1,0:T(8,128)(2,1)S(1)} %constant_dynamic-update-slice_fusion.refs_0_), channel_id=1, source_target_pairs={{0,64},{64,0},{1,65},{65,1},{2,66},{66,2},{3,67},{67,3},{4,68},{68... | collective-permute-start | bytes 2359304 | tf_op jit(solution)/shard_map/ppermute | solution.py:276
  34.8 1.2 copy-start
  36.0 0.9 copy-start.1
  37.0 0.7 copy-start.6
  48.3 51.4 %copy-start.8 = (bf16[1024,384]{1,0:T(8,128)(2,1)}, bf16[1024,384]{1,0:T(8,128)(2,1)S(1)}, u32[]{:S(2)}) copy-start(bf16[1024,384]{1,0:T(8,128)(2,1)S(1)} %collective-permute-done.2.refs_1_) | copy-start | bytes 2359300
  50.9 48.8 %copy-start.9 = (bf16[1024,384]{1,0:T(8,128)(2,1)}, bf16[1024,384]{1,0:T(8,128)(2,1)S(1)}, u32[]{:S(2)}) copy-start(bf16[1024,384]{1,0:T(8,128)(2,1)S(1)} %collective-permute-done.3.refs_2_) | copy-start | bytes 2359300
  54.4 63.7 %copy-start.4 = (f32[7,3,128]{2,0,1:T(8,128)S(1)}, f32[7,3,128]{2,0,1:T(8,128)}, u32[]{:S(2)}) copy-start(f32[7,3,128]{2,0,1:T(8,128)} %param.14) | copy-start | bytes 32260
  54.4 63.7 %copy-start.5 = (f32[128,16]{0,1:T(8,128)S(1)}, f32[128,16]{0,1:T(8,128)}, u32[]{:S(2)}) copy-start(f32[128,16]{0,1:T(8,128)} %param.16) | copy-start | bytes 24580
  54.4 63.7 %copy-start.7 = (f32[128]{0:T(128)S(1)}, f32[128]{0:T(128)}, u32[]{:S(2)}) copy-start(f32[128]{0:T(128)} %param.17) | copy-start | bytes 1540
  54.4 23.4 %collective-permute-start.5 = (bf16[512,384]{1,0:T(8,128)(2,1)S(1)}, bf16[512,384]{1,0:T(8,128)(2,1)S(1)}, u32[]{:S(2)}, u32[]{:S(2)}) collective-permute-start(bf16[512,384]{1,0:T(8,128)(2,1)S(1)} %slice.12), channel_id=1, source_target_pairs={{0,128},{128,256},{256,384},{384,0},{1,129},{129,257},{257,385},{3... | collective-permute-start | bytes 1179656 | tf_op jit(solution)/shard_map/ppermute | solution.py:238
  56.8 21.0 %collective-permute-start.6 = (bf16[512,384]{1,0:T(8,128)(2,1)S(1)}, bf16[512,384]{1,0:T(8,128)(2,1)S(1)}, u32[]{:S(2)}, u32[]{:S(2)}) collective-permute-start(bf16[512,384]{1,0:T(8,128)(2,1)S(1)} %slice.13), channel_id=1, source_target_pairs={{0,384},{128,0},{256,128},{384,256},{1,385},{129,1},{257,129},{385... | collective-permute-start | bytes 1179656 | tf_op jit(solution)/shard_map/ppermute | solution.py:238
  61.7 37.9 %collective-permute-start.8 = (bf16[1024,384]{1,0:T(8,128)(2,1)}, bf16[1024,384]{1,0:T(8,128)(2,1)}, u32[]{:S(2)}, u32[]{:S(2)}) collective-permute-start(bf16[1024,384]{1,0:T(8,128)(2,1)} %collective-permute-done.4.refs_5_), channel_id=1, source_target_pairs={{0,128},{128,256},{256,384},{384,0},{1,129},{129,257},{257,385},{3... | collective-permute-start | bytes 2359304 | tf_op jit(solution)/shard_map/ppermute | solution.py:286
  63.6 36.0 %collective-permute-start.9 = (bf16[1024,384]{1,0:T(8,128)(2,1)}, bf16[1024,384]{1,0:T(8,128)(2,1)}, u32[]{:S(2)}, u32[]{:S(2)}) collective-permute-start(bf16[1024,384]{1,0:T(8,128)(2,1)} %collective-permute-done.4.refs_5_), channel_id=1, source_target_pairs={{0,384},{128,0},{256,128},{384,256},{1,385},{129,1},{257,129},{385... | collective-permute-start | bytes 2359304 | tf_op jit(solution)/shard_map/ppermute | solution.py:286
  68.8 8.4 %collective-permute-start.7 = (f32[16,16,128]{2,1,0:T(8,128)S(1)}, f32[16,16,128]{2,1,0:T(8,128)S(1)}, u32[]{:S(2)}, u32[]{:S(2)}) collective-permute-start(f32[16,16,128]{2,1,0:T(8,128)S(1)} %slice.15), channel_id=1, source_target_pairs={{0,16},{16,0},{1,17},{17,1},{2,18},{18,2},{3,19},{19,3},{4,20},{20... | collective-permute-start | bytes 393224 | tf_op jit(solution)/shard_map/ppermute | solution.py:285
  77.8 21.9 %copy-start.11 = (bf16[512,384]{1,0:T(8,128)(2,1)}, bf16[512,384]{1,0:T(8,128)(2,1)S(1)}, u32[]{:S(2)}) copy-start(bf16[512,384]{1,0:T(8,128)(2,1)S(1)} %collective-permute-done.5.refs_3_) | copy-start | bytes 1179652
  77.8 21.9 %copy-start.12 = (bf16[512,384]{1,0:T(8,128)(2,1)}, bf16[512,384]{1,0:T(8,128)(2,1)S(1)}, u32[]{:S(2)}) copy-start(bf16[512,384]{1,0:T(8,128)(2,1)S(1)} %collective-permute-done.6.refs_4_) | copy-start | bytes 1179652
  77.8 21.8 %collective-permute-start.10 = (bf16[512,384]{1,0:T(8,128)(2,1)S(1)}, bf16[512,384]{1,0:T(8,128)(2,1)}, u32[]{:S(2)}, u32[]{:S(2)}) collective-permute-start(bf16[512,384]{1,0:T(8,128)(2,1)S(1)} %collective-permute-done.5.refs_3_), channel_id=1, source_target_pairs={{0,64},{64,0},{1,65},{65,1},{2,66},{66,2},{3,67},{67,3},{4,68},{68... | collective-permute-start | bytes 1179656 | tf_op jit(solution)/shard_map/ppermute | solution.py:288
  80.3 19.3 %collective-permute-start.11 = (bf16[512,384]{1,0:T(8,128)(2,1)S(1)}, bf16[512,384]{1,0:T(8,128)(2,1)}, u32[]{:S(2)}, u32[]{:S(2)}) collective-permute-start(bf16[512,384]{1,0:T(8,128)(2,1)S(1)} %collective-permute-done.6.refs_4_), channel_id=1, source_target_pairs={{0,64},{64,0},{1,65},{65,1},{2,66},{66,2},{3,67},{67,3},{4,68},{68... | collective-permute-start | bytes 1179656 | tf_op jit(solution)/shard_map/ppermute | solution.py:288
  84.4 27.7 %all-to-all-start = ((f32[16,16,128]{2,1,0:T(8,128)}), f32[16,16,128]{2,1,0:T(8,128)S(1)}, u32[]{:S(2)}, u32[]{:S(2)}) async-start(f32[16,16,128]{2,1,0:T(8,128)} %slice_add_fusion), calls=%async_computation | async-start | bytes 262144 | tf_op jit(solution)/shard_map/all_to_all | solution.py:290
  107.3 4.9 %collective-permute-start.12 = (bf16[256,384]{1,0:T(8,128)(2,1)}, bf16[256,384]{1,0:T(8,128)(2,1)S(1)}, u32[]{:S(2)}, u32[]{:S(2)}) collective-permute-start(bf16[256,384]{1,0:T(8,128)(2,1)} %get-tuple-element.26), channel_id=1, source_target_pairs={{0,0},{16,32},{32,16},{48,48},{1,1},{17,33},{33,17},{49,49},{2,2},... | collective-permute-start | bytes 589832 | tf_op jit(solution)/shard_map/ppermute | solution.py:272
  108.8 9.3 %collective-permute-start.13 = (bf16[256,384]{1,0:T(8,128)(2,1)}, bf16[256,384]{1,0:T(8,128)(2,1)S(1)}, u32[]{:S(2)}, u32[]{:S(2)}) collective-permute-start(bf16[256,384]{1,0:T(8,128)(2,1)} %get-tuple-element.27), channel_id=1, source_target_pairs={{0,32},{16,0},{32,48},{48,16},{1,33},{17,1},{33,49},{49,17},{2,34}... | collective-permute-start | bytes 589832 | tf_op jit(solution)/shard_map/ppermute | solution.py:272
Sparse Core Ops, SparseCore 0:
  9.9 83.4 all-gather.2
